TPU v7x, 256 devices: a whole 4x4x8 slice. The times are simulated.
256 devices in a mesh: dp: 32 (over y, z), expert: 8 (over x, core).
Axes of the slice: x: 4, y: 4, z: 8, core: 2. Of those that a mesh axis runs over, the one named last changes fastest.
Arguments:
- tokens: bfloat16 [2048, 3072], P('expert'), may hold values from -6 to 6
- cotangent: bfloat16 [2048, 3072], P('expert'), may hold values from -6 to 6
- routes: int32 [2048, 2], P('expert'), may hold values from 0 to 7, all different within a row; in each aligned block of 256 rows (0 to 255, 256 to 511, ...) at most 128 rows name the same one
- gate_values: bfloat16 [2048, 2], P('expert'), may hold values from 0.049804688 to 0.94921875
- gate_weight: bfloat16 [8, 3072, 8192], P('expert', None, 'dp'), may hold values from -0.109375 to 0.109375
- up_weight: bfloat16 [8, 3072, 8192], P('expert', None, 'dp'), may hold values from -0.109375 to 0.109375
- down_weight: bfloat16 [8, 3072, 8192], P('expert', None, 'dp'), may hold values from -0.0625 to 0.0625
Outputs:
- clipped: bfloat16 [8, 3, 3072, 8192], P('expert', None, 'dp')
- d_tokens: bfloat16 [3072, 2048], P('dp', 'expert')
Inputs may be any that keep to these rules, and one draw needn't show every extreme that they name: `routes`: each row names two different experts. Within the 256 rows of one device along expert (aligned blocks), no expert is named by more than 128 rows.
All inputs are finite; a program needn't handle non-finite values.
Results may differ from a plain program's by a relative error of at most 0.0064.
Values may be sent and summed in bfloat16 or wider, within the bound.
A program may use at most 128 MiB of HBM per device.

v0:
```python
import math

import jax
import jax.numpy as jnp
from jax import lax
from jax.sharding import PartitionSpec as P

CAP = 128


CLIP_RMS = 0.2


def slots_of(route_block, experts):
    flat_routes = route_block.reshape(-1)
    onehot = (flat_routes[:, None] == jnp.arange(experts, dtype=jnp.int32)[None, :]).astype(
        jnp.int32
    )
    before = jnp.cumsum(onehot, axis=0) - onehot
    position = jnp.sum(before * onehot, axis=1)
    counts = jnp.sum(onehot, axis=0)
    return (flat_routes * CAP + position, counts)


def fill_rows(token_block, cot_block, gate_block, slot_index, counts, experts):
    routed = slot_index.shape[0]
    row_of_slot = (
        jnp.zeros((experts * CAP,), jnp.int32)
        .at[slot_index]
        .set(jnp.arange(routed, dtype=jnp.int32))
    )
    live_slot = (jnp.arange(CAP, dtype=jnp.int32)[None, :] < counts[:, None]).reshape(-1)
    token_of_slot = row_of_slot // 2
    input_rows = jnp.where(
        live_slot[:, None], token_block[token_of_slot], jnp.zeros((), token_block.dtype)
    )
    scaled = gate_block.reshape(-1)[row_of_slot].astype(jnp.float32)[:, None] * cot_block[
        token_of_slot
    ].astype(jnp.float32)
    weighted_rows = jnp.where(live_slot[:, None], scaled, jnp.zeros((), scaled.dtype)).astype(
        jnp.bfloat16
    )
    model_width = token_block.shape[1]
    return (
        input_rows.reshape(experts, CAP, model_width),
        weighted_rows.reshape(experts, CAP, model_width),
    )


def row_contract(left, right):
    return lax.dot_general(
        left, right, (((0,), (0,)), ((), ())), preferred_element_type=jnp.float32
    )


def unit_contract(left, right):
    return lax.dot_general(
        left, right, (((1,), (1,)), ((), ())), preferred_element_type=jnp.float32
    )


def expert_pass(input_rows, weighted_rows, gate_matrix, up_matrix, down_matrix):
    pre_gate = jnp.dot(input_rows, gate_matrix, preferred_element_type=jnp.float32)
    pre_up = jnp.dot(input_rows, up_matrix, preferred_element_type=jnp.float32)
    sigmoid_gate = jax.nn.sigmoid(pre_gate)
    activated = pre_gate * sigmoid_gate
    hidden = (activated * pre_up).astype(jnp.bfloat16)
    grad_hidden = jnp.dot(weighted_rows, down_matrix, preferred_element_type=jnp.float32)
    grad_gate = (
        grad_hidden * pre_up * sigmoid_gate * (1.0 + pre_gate * (1.0 - sigmoid_gate))
    ).astype(jnp.bfloat16)
    grad_up = (grad_hidden * activated).astype(jnp.bfloat16)
    stacked = jnp.stack(
        [
            row_contract(input_rows, grad_gate),
            row_contract(input_rows, grad_up),
            row_contract(weighted_rows, hidden),
        ]
    )
    return (stacked, grad_gate, grad_up)


def per_device(tokens, cotangent, routes, gate_values, gate_weight, up_weight, down_weight):
    experts = lax.axis_size("expert")
    shards = lax.axis_size("dp")
    model_width = tokens.shape[1]
    gate_matrix = gate_weight[0]
    up_matrix = up_weight[0]
    down_matrix = down_weight[0]
    units = gate_matrix.shape[1]
    slot_index, counts = slots_of(routes, experts)
    input_send, weighted_send = fill_rows(
        tokens, cotangent, gate_values, slot_index, counts, experts
    )
    input_recv, weighted_recv, counts_recv = (
        lax.all_to_all(input_send, "expert", split_axis=0, concat_axis=0, tiled=True),
        lax.all_to_all(weighted_send, "expert", split_axis=0, concat_axis=0, tiled=True),
        lax.all_to_all(counts, "expert", split_axis=0, concat_axis=0, tiled=True),
    )
    slot_total = experts * CAP
    input_rows = input_recv.reshape(slot_total, model_width)
    weighted_rows = weighted_recv.reshape(slot_total, model_width)
    grad_sum, grad_gate, grad_up = expert_pass(
        input_rows, weighted_rows, gate_matrix, up_matrix, down_matrix
    )
    summed = lax.psum_scatter(
        unit_contract(gate_matrix, grad_gate) + unit_contract(up_matrix, grad_up),
        "dp",
        scatter_dimension=0,
        tiled=True,
    )
    returned_rows = lax.all_to_all(summed, "expert", split_axis=1, concat_axis=1, tiled=True)
    picked = returned_rows[:, slot_index]
    d_tokens = jnp.sum(picked.reshape(picked.shape[0], slot_index.shape[0] // 2, 2), axis=2).astype(
        jnp.bfloat16
    )
    gradients = grad_sum.astype(jnp.bfloat16)
    owned_rows = lax.all_to_all(gradients, "dp", split_axis=1, concat_axis=2, tiled=True)
    squares = lax.psum(jnp.sum(jnp.square(owned_rows.astype(jnp.float32))), ("dp", "expert"))
    clip_limit = CLIP_RMS * math.sqrt(3.0 * experts * model_width * units * shards)
    clip_scale = clip_limit / jnp.maximum(jnp.sqrt(squares), clip_limit)
    clipped = (owned_rows.astype(jnp.float32) * clip_scale).astype(jnp.bfloat16)
    return (clipped[None], d_tokens)


def solution(mesh):
    return jax.shard_map(
        per_device,
        mesh=mesh,
        in_specs=(
            P("expert", None),
            P("expert", None),
            P("expert", None),
            P("expert", None),
            P("expert", None, "dp"),
            P("expert", None, "dp"),
            P("expert", None, "dp"),
        ),
        out_specs=(P("expert", None, "dp", None), P("dp", "expert")),
        check_vma=False,
    )
```

profile of v0, /device:TPU:12, one launch (start us, length us, event | category | flops | bytes accessed | tf_op | source)
XLA Modules:
  0.0 572.3 jit_solution(8340505373630688563)
XLA Ops:
  9.4 1.1 reduce-window.6
  11.0 2.4 scatter_custom_fusion
  13.5 13.8 %gather_fusion = bf16[1024,3072]{1,0:T(8,128)(2,1)} fusion(bf16[256,3072]{1,0:T(8,128)(2,1)} %param.7, s32[1024]{0:T(1024)S(1)} %get-tuple-element.9), kind=kCustom, calls=%fused_computation | custom fusion | bytes 12587008 | tf_op jit(solution)/shard_map/gather | solution.py:35
  27.3 5.9 %broadcast_select_fusion = bf16[8,128,3072]{2,1,0:T(8,128)(2,1)} fusion(bf16[8,128,3072]{2,1,0:T(8,128)(2,1)} %bitcast.59, pred[8,128]{1,0:T(8,128)(4,1)S(1)} %iota_compare_fusion.2), kind=kLoop, calls=%fused_computation.13 | loop fusion | flops 3145728 | bytes 12583936 | tf_op jit(solution)/shard_map/jit(_where)/select_n | solution.py:34
  33.2 5.3 all-to-all-start
  38.6 6.8 %gather_fusion.2 = bf16[1024,3072]{1,0:T(8,128)(2,1)} fusion(bf16[256,3072]{1,0:T(8,128)(2,1)S(1)} %copy-done.2, s32[1024]{0:T(1024)S(1)} %get-tuple-element.9), kind=kCustom, calls=%fused_computation.2 | custom fusion | bytes 12587008 | tf_op jit(solution)/shard_map/gather | solution.py:37
  45.7 6.8 %gather_fusion.1 = bf16[1024]{0:T(1024)(128)(2,1)S(1)} fusion(bf16[512]{0:T(512)(128)(2,1)S(1)} %reshape.131, s32[1024]{0:T(1024)S(1)} %get-tuple-element.8), kind=kCustom, calls=%fused_computation.1 | custom fusion | bytes 8192 | tf_op jit(solution)/shard_map/gather | solution.py:37
  52.5 8.9 %fusion.3 = bf16[8,128,3072]{2,1,0:T(8,128)(2,1)} fusion(bf16[8,128,3072]{2,1,0:T(8,128)(2,1)} %bitcast.58, f32[8,128]{1,0:T(8,128)S(1)} %bitcast_convert_fusion, pred[8,128]{1,0:T(8,128)(4,1)S(1)} %iota_compare_fusion.2), kind=kLoop, calls=%fused_computation.11 | loop fusion | flops 12582912 | bytes 12588032 | tf_op jit(solution)/shard_map/convert_element_type | solution.py:40
  61.5 46.1 %all-to-all-done = bf16[8,128,3072]{2,1,0:T(8,128)(2,1)} async-done(((bf16[8,128,3072]{2,1,0:T(8,128)(2,1)}), bf16[8,128,3072]{2,1,0:T(8,128)(2,1)}, u32[]{:S(2)}, u32[]{:S(2)}) %all-to-all-start) | async-done | bytes 6291488 | tf_op jit(solution)/shard_map/all_to_all | solution.py:96
  107.6 7.8 %all-to-all-start.1 = ((bf16[8,128,3072]{2,1,0:T(8,128)(2,1)}), bf16[8,128,3072]{2,1,0:T(8,128)(2,1)}, u32[]{:S(2)}, u32[]{:S(2)}) async-start(bf16[8,128,3072]{2,1,0:T(8,128)(2,1)} %fusion.3), calls=%async_computation.1 | async-start | bytes 12582912 | tf_op jit(solution)/shard_map/all_to_all | solution.py:97
  115.5 5.5 fusion.12
  121.0 63.5 %all-to-all-done.1 = bf16[8,128,3072]{2,1,0:T(8,128)(2,1)} async-done(((bf16[8,128,3072]{2,1,0:T(8,128)(2,1)}), bf16[8,128,3072]{2,1,0:T(8,128)(2,1)}, u32[]{:S(2)}, u32[]{:S(2)}) %all-to-all-start.1) | async-done | bytes 6291488 | tf_op jit(solution)/shard_map/all_to_all | solution.py:97
  184.5 5.1 fusion.14
  189.7 5.8 %multiply_convert_fusion.2 = (bf16[1024,256]{1,0:T(8,128)(2,1)S(1)}, bf16[1024,256]{1,0:T(8,128)(2,1)S(1)}, f32[1024,256]{1,0:T(8,128)}) fusion(f32[1024,256]{1,0:T(8,128)S(1)} %fusion.14, f32[1024,256]{1,0:T(8,128)S(1)} %copy-done.7, bf16[1024,3072]{1,0:T(8,128)(2,1)} %bitcast.5, bf16[1,3072,256]{2,1,0:T(8,128)(2,1)S(1)} %copy-done), kind=kOutput, calls=%fused_computation.32 | convolution fusion | flops 1614020608 | bytes 12058624 | tf_op jit(solution)/shard_map/dot_general | solution.py:63
  195.4 1.8 fusion.7
  197.3 6.3 %add_bitcast_fusion = f32[3072,1024]{0,1:T(8,128)} fusion(f32[1024,3072]{1,0:T(8,128)S(1)} %fusion.7, bf16[1024,256]{1,0:T(8,128)(2,1)S(1)} %get-tuple-element.7, bf16[1,3072,256]{2,1,0:T(8,128)(2,1)S(1)} %copy-done.5), kind=kOutput, calls=%fused_computation.12 | convolution fusion | flops 1613758464 | bytes 27262976 | tf_op jit(solution)/shard_map/dot_general | solution.py:57
  203.6 12.6 %copy.24 = f32[3072,1024]{1,0:T(8,128)} copy(f32[3072,1024]{0,1:T(8,128)} %add_bitcast_fusion) | data formatting | bytes 25165824
  216.2 4.7 fusion.5
  220.9 4.8 fusion.4
  225.7 4.9 fusion.6
  231.2 23.9 %copy.19 = bf16[3,3072,256]{2,0,1:T(4,128)(2,1)S(1)} copy(bf16[3,3072,256]{2,1,0:T(8,128)(2,1)S(1)} %pad_maximum_fusion) | data formatting | bytes 9437184 | tf_op jit(solution)/shard_map/stack | solution.py:73
  255.2 189.4 %all_to_all.31 = bf16[3,3072,256]{2,0,1:T(4,128)(2,1)S(1)} all-to-all(bf16[3,3072,256]{2,0,1:T(4,128)(2,1)S(1)} %copy.19), channel_id=1, replica_groups=mesh['dp'=32,'expert'=8] {'dp'}, dimensions={1} | all-to-all | bytes 9437184 | tf_op jit(solution)/shard_map/all_to_all | solution.py:118
  444.6 2.6 copy-done.3
  447.2 7.1 %fusion = f32[]{:T(128)} fusion(bf16[3,3072,256]{2,0,1:T(4,128)(2,1)S(1)} %all_to_all.31), kind=kLoop, calls=%fused_computation.7 | loop fusion | flops 7077887 | bytes 4718596 | tf_op jit(solution)/shard_map/reduce_sum | solution.py:119
  454.3 74.6 %psum.7 = f32[]{:T(128)} all-reduce(f32[]{:T(128)} %fusion), channel_id=1, replica_groups=mesh['dp'=32,'expert'=8] {'dp','expert'}, use_global_device_ids=true, to_apply=%region_6.7 | all-reduce | flops 1 | bytes 8 | tf_op jit(solution)/shard_map/psum | solution.py:119
  529.7 7.1 %reduce-scatter.4.cloned.1.call-done = f32[96,1024]{1,0:T(8,128)} async-done(((f32[3072,1024]{1,0:T(8,128)}), f32[96,1024]{1,0:T(8,128)}) %reduce-scatter.4.cloned.1.call-update) | async-done | bytes 393232
  536.7 1.2 copy.25
  538.9 4.8 all-to-all-start.3
  543.7 5.5 fusion.1
  549.2 5.6 copy.20
  554.8 8.3 %convert_element_type.84 = bf16[1,3,96,8192]{3,2,1,0:T(8,128)(2,1)} reshape(bf16[3,96,32,256]{3,2,1,0:T(8,128)(2,1)} %copy.20) | data formatting | bytes 9437184 | tf_op jit(solution)/shard_map/convert_element_type | solution.py:122
  563.3 1.0 gather_fusion.3
  (46 shorter events, 5.9 us)
Async XLA Ops:
  7.2 182.5 %copy-start = (bf16[1,3072,256]{2,1,0:T(8,128)(2,1)S(1)}, bf16[1,3072,256]{2,1,0:T(8,128)(2,1)}, u32[]{:S(2)}) copy-start(bf16[1,3072,256]{2,1,0:T(8,128)(2,1)} %param.11) | copy-start | bytes 4718596
  33.2 5.3 copy-start.2
  33.2 74.4 %all-to-all-start = ((bf16[8,128,3072]{2,1,0:T(8,128)(2,1)}), bf16[8,128,3072]{2,1,0:T(8,128)(2,1)}, u32[]{:S(2)}, u32[]{:S(2)}) async-start(bf16[8,128,3072]{2,1,0:T(8,128)(2,1)} %broadcast_select_fusion), calls=%async_computation | async-start | bytes 12582912 | tf_op jit(solution)/shard_map/all_to_all | solution.py:96
  38.6 6.8 %copy-start.6 = (bf16[256,2]{0,1:T(2,128)(2,1)S(1)}, bf16[256,2]{0,1:T(2,128)(2,1)}, u32[]{:S(2)}) copy-start(bf16[256,2]{0,1:T(2,128)(2,1)} %param.10) | copy-start | bytes 3076
  61.5 54.0 %copy-start.4 = (bf16[1,3072,256]{2,1,0:T(8,128)(2,1)S(1)}, bf16[1,3072,256]{2,1,0:T(8,128)(2,1)}, u32[]{:S(2)}) copy-start(bf16[1,3072,256]{2,1,0:T(8,128)(2,1)} %param.12) | copy-start | bytes 4718596
  107.6 76.9 %all-to-all-start.1 = ((bf16[8,128,3072]{2,1,0:T(8,128)(2,1)}), bf16[8,128,3072]{2,1,0:T(8,128)(2,1)}, u32[]{:S(2)}, u32[]{:S(2)}) async-start(bf16[8,128,3072]{2,1,0:T(8,128)(2,1)} %fusion.3), calls=%async_computation.1 | async-start | bytes 12582912 | tf_op jit(solution)/shard_map/all_to_all | solution.py:97
  115.5 421.3 %reduce-scatter.4.cloned.1.call-start = ((), (), s32[]{:S(2)}) async-start(), calls=%async_computation.5 | async-start | bytes 12976128
  184.5 5.1 copy-start.7
  195.4 1.8 copy-start.5
  220.9 4.8 copy-start.8
  220.9 4.8 copy-start.9
  444.6 2.6 copy-start.3
  538.9 24.2 %all-to-all-start.3 = ((f32[96,8,128]{2,0,1:T(8,128)}), f32[96,8,128]{2,0,1:T(8,128)S(1)}, u32[]{:S(2)}, u32[]{:S(2)}) async-start(f32[96,8,128]{2,0,1:T(8,128)} %copy.21), calls=%async_computation.3 | async-start | bytes 786432 | tf_op jit(solution)/shard_map/all_to_all | solution.py:112
  549.2 16.3 %copy-start.1 = (bf16[1,3072,256]{2,1,0:T(8,128)(2,1)S(1)}, bf16[1,3072,256]{2,1,0:T(8,128)(2,1)}, u32[]{:S(2)}) copy-start(bf16[1,3072,256]{2,1,0:T(8,128)(2,1)} %param.11) | copy-start | bytes 4718596
Sparse Core Ops, SparseCore 0:
  216.3 320.3 reduce-scatter.3
where the time goes:
time: 575 us; the launch traced here: 572 us
  blocking collectives  264 us (46%)
  waiting for transfers between devices  117 us (20%)
  local copies, waits for them, and re-layouts  88.9 us (15%)
  matrix products  39 us (7%)
  other arithmetic  30.7 us (5%)
  starting transfers between devices  18 us (3%)
  between operations  15 us (3%)
    all_to_all x1, blocking collectives, per_device(): lax.all_to_all(gradients, 'dp', split_axis=1, concat_axis=2, tiled=True)  189 us
    psum x1, blocking collectives, per_device(): lax.psum(jnp.sum(jnp.square(owned_rows.astype(jnp.float32))), ('dp', 'exp...  74.6 us
    all_to_all x1, waiting for transfers between devices, per_device(): lax.all_to_all(weighted_send, 'expert', split_axis=0, concat_axis=0, tile...  63.5 us
    all_to_all x1, waiting for transfers between devices, per_device(): lax.all_to_all(input_send, 'expert', split_axis=0, concat_axis=0, tiled=T...  46.1 us
    another operation x1, local copies, waits for them, and re-layouts, expert_pass(): jnp.stack([row_contract(input_rows, grad_gate), row_contract(input_rows,...  23.9 us
    unnamed x25, local copies, waits for them, and re-layouts  18.1 us
    dot_general x3, matrix products, row_contract(): lax.dot_general(left, right, (((0,), (0,)), ((), ())), preferred_element_...  14.4 us
    convert_element_type x2, local copies, waits for them, and re-layouts, per_device(): clipped = (owned_rows.astype(jnp.float32) * clip_scale).astype(jnp.bfloat16)  13.9 us
  transfers between devices with their start and end apart: 4, of which 3 were waited for; matrix products, arithmetic and copies ran while one was open for 16% of the time, Pallas kernels for 0%

commit v1 on v0

v1 whole, which is shorter than its diff:
```python
import functools
import math

import jax
import jax.numpy as jnp
from jax import lax
from jax.experimental import pallas as pl
from jax.experimental.pallas import tpu as pltpu
from jax.sharding import PartitionSpec as P

CAP = 128
CLIP_RMS = 0.2
MESH = pl.DeviceIdType.MESH
F32 = jnp.float32
BF16 = jnp.bfloat16


def slot_match(routes, experts):
    flat = routes.reshape(-1)
    pairs = flat.shape[0]
    onehot = flat[:, None] == jnp.arange(experts, dtype=jnp.int32)[None, :]
    earlier = jnp.arange(pairs)[None, :] < jnp.arange(pairs)[:, None]
    before = jnp.dot(earlier.astype(BF16), onehot.astype(BF16), preferred_element_type=F32)
    position = jnp.sum(jnp.where(onehot, before, 0.0), axis=1).astype(jnp.int32)
    slot = (flat * CAP + position).reshape(routes.shape)
    slots = jnp.arange(experts * CAP, dtype=jnp.int32)[:, None]
    return slots == slot[:, 0][None, :], slots == slot[:, 1][None, :]


def kernel(
    shape,
    x_ref, w_ref, gate_ref, up_ref, down_ref, pick_ref,
    clip_ref, tok_ref,
    h_ref, g_ref, row_send, row_recv, grad_send, grad_recv,
    y_send, y_recv, z_send, z_recv, sq_ref, sq_dp, sq_ex,
    row_ss, row_rs, grad_ss, grad_rs, y_ss, y_rs, z_ss, z_rs, sd_ss, sd_rs, se_ss, se_rs,
):
    ny, nz, experts, limit = shape
    shards = ny * nz
    dp = lax.axis_index("dp")
    ex = lax.axis_index("expert")
    my_y, my_z = dp // nz, lax.rem(dp, nz)
    slots, width = x_ref.shape
    units = gate_ref.shape[1]
    own = width // shards
    group = own * 4
    groups = shards // 4
    tile = slots // experts

    barrier = pltpu.get_barrier_semaphore()

    def greet_dp(k, _):
        pl.semaphore_signal(
            barrier, inc=1, device_id=(lax.rem(dp + k, shards), ex), device_id_type=MESH
        )
        return 0

    def greet_ex(k, _):
        pl.semaphore_signal(
            barrier, inc=1, device_id=(dp, lax.rem(ex + k, experts)), device_id_type=MESH
        )
        return 0

    lax.fori_loop(1, shards, greet_dp, 0)
    lax.fori_loop(1, experts, greet_ex, 0)
    pl.semaphore_wait(barrier, shards + experts - 2)

    chunk = 256

    def hidden(i, _):
        rows = pl.ds(pl.multiple_of(i * chunk, chunk), chunk)
        pre_gate = jnp.dot(x_ref[rows, :], gate_ref[...], preferred_element_type=F32)
        pre_up = jnp.dot(x_ref[rows, :], up_ref[...], preferred_element_type=F32)
        grad_hidden = jnp.dot(w_ref[rows, :], down_ref[...], preferred_element_type=F32)
        s = jax.nn.sigmoid(pre_gate)
        act = pre_gate * s
        h_ref[rows, :] = (act * pre_up).astype(BF16)
        g_ref[rows, :units] = (
            grad_hidden * pre_up * s * (1.0 + pre_gate * (1.0 - s))
        ).astype(BF16)
        g_ref[rows, units:] = (grad_hidden * act).astype(BF16)
        return 0

    lax.fori_loop(0, slots // chunk, hidden, 0)

    def row_copy(e):
        return pltpu.make_async_remote_copy(
            src_ref=row_send.at[e], dst_ref=row_recv.at[ex],
            send_sem=row_ss.at[e], recv_sem=row_rs.at[ex],
            device_id=(dp, e), device_id_type=MESH,
        )

    def row_arrival(e):
        return pltpu.make_async_remote_copy(
            src_ref=row_send.at[e], dst_ref=row_recv.at[e],
            send_sem=row_ss.at[e], recv_sem=row_rs.at[e],
            device_id=(dp, e), device_id_type=MESH,
        )

    pairs = experts // 2
    part = width // ny

    def row_pair(k, _):
        c = lax.rem(ex // 2 + pairs - 1 - k, pairs)
        rows = pl.ds(pl.multiple_of(c * 2 * tile, 2 * tile), 2 * tile)
        e0 = 2 * c

        def piece(m, _):
            feats = pl.ds(pl.multiple_of(m * part, part), part)
            got = lax.dot_general(
                gate_ref[feats, :], g_ref[rows, :units], (((1,), (1,)), ((), ())),
                preferred_element_type=F32,
            ) + lax.dot_general(
                up_ref[feats, :], g_ref[rows, units:], (((1,), (1,)), ((), ())),
                preferred_element_type=F32,
            )
            got = got.astype(BF16)
            row_send[e0, feats, :] = got[:, :tile]
            row_send[e0 + 1, feats, :] = got[:, tile:]
            return 0

        lax.fori_loop(0, ny, piece, 0)
        for i in range(2):
            @pl.when(e0 + i != ex)
            def _():
                row_copy(e0 + i).start()
        return 0

    lax.fori_loop(0, pairs, row_pair, 0)

    def grad_copy(p):
        return pltpu.make_async_remote_copy(
            src_ref=grad_send.at[p], dst_ref=grad_recv.at[dp],
            send_sem=grad_ss.at[p], recv_sem=grad_rs.at[dp],
            device_id=(p, ex), device_id_type=MESH,
        )

    def grad_arrival(p):
        return pltpu.make_async_remote_copy(
            src_ref=grad_send.at[p], dst_ref=grad_recv.at[p],
            send_sem=grad_ss.at[p], recv_sem=grad_rs.at[p],
            device_id=(p, ex), device_id_type=MESH,
        )

    sq_ref[...] = jnp.zeros_like(sq_ref)

    def grad_group(k, _):
        c = lax.rem(dp // 4 + k, groups)
        feats = pl.ds(pl.multiple_of(c * group, group), group)
        total = jnp.zeros(sq_ref.shape, F32)
        first = lax.dot_general(
            x_ref[:, feats], g_ref[...], (((0,), (0,)), ((), ())), preferred_element_type=F32
        ).astype(BF16)
        last = lax.dot_general(
            w_ref[:, feats], h_ref[...], (((0,), (0,)), ((), ())), preferred_element_type=F32
        ).astype(BF16)
        for i in range(4):
            rows = slice(i * own, (i + 1) * own)
            for m, block in enumerate((first[rows, :units], first[rows, units:], last[rows, :])):
                grad_send[4 * c + i, m] = block
                wide = block.astype(F32)
                wide = wide * wide
                total += jnp.sum(wide.reshape(own // 8, 8, units), axis=0)
        sq_ref[...] += total
        for i in range(4):
            @pl.when(4 * c + i != dp)
            def _():
                grad_copy(4 * c + i).start()
        return 0

    lax.fori_loop(0, groups, grad_group, 0)

    def sd_copy(k):
        p = lax.rem(dp + k, shards)
        return pltpu.make_async_remote_copy(
            src_ref=sq_ref, dst_ref=sq_dp.at[dp], send_sem=sd_ss.at[k], recv_sem=sd_rs.at[dp],
            device_id=(p, ex), device_id_type=MESH,
        )

    def sd_arrival(k):
        p = lax.rem(dp + k, shards)
        return pltpu.make_async_remote_copy(
            src_ref=sq_ref, dst_ref=sq_dp.at[p], send_sem=sd_ss.at[k], recv_sem=sd_rs.at[p],
            device_id=(p, ex), device_id_type=MESH,
        )

    def se_copy(k):
        p = lax.rem(ex + k, experts)
        return pltpu.make_async_remote_copy(
            src_ref=sq_dp.at[dp], dst_ref=sq_ex.at[ex], send_sem=se_ss.at[k],
            recv_sem=se_rs.at[ex], device_id=(dp, p), device_id_type=MESH,
        )

    def se_arrival(k):
        p = lax.rem(ex + k, experts)
        return pltpu.make_async_remote_copy(
            src_ref=sq_dp.at[dp], dst_ref=sq_ex.at[p], send_sem=se_ss.at[k],
            recv_sem=se_rs.at[p], device_id=(dp, p), device_id_type=MESH,
        )

    def run(first, count, do):
        def body(k, _):
            do(k)
            return 0
        lax.fori_loop(first, count, body, 0)

    run(1, shards, lambda k: sd_copy(k).start())
    run(1, shards, lambda k: sd_arrival(k).wait())

    def add_dp(k, total):
        return total + sq_dp[lax.rem(dp + k, shards)]

    sq_dp[dp] = lax.fori_loop(1, shards, add_dp, sq_ref[...])
    sq_ex[ex] = sq_dp[dp]
    run(1, experts, lambda k: se_copy(k).start())

    row_recv[ex] = row_send[ex]

    def y_copy(k):
        p = lax.rem(my_y + k, ny)
        return pltpu.make_async_remote_copy(
            src_ref=y_send.at[p], dst_ref=y_recv.at[my_y], send_sem=y_ss.at[p],
            recv_sem=y_rs.at[my_y], device_id=(p * nz + my_z, ex), device_id_type=MESH,
        )

    def y_arrival(k):
        p = lax.rem(my_y + k, ny)
        return pltpu.make_async_remote_copy(
            src_ref=y_send.at[p], dst_ref=y_recv.at[p], send_sem=y_ss.at[p],
            recv_sem=y_rs.at[p], device_id=(p * nz + my_z, ex), device_id_type=MESH,
        )

    def wait_row(k):
        row_arrival(lax.rem(ex + k, experts)).wait()

    run(1, experts, wait_row)

    def to_tokens(k, _):
        p = lax.rem(my_y + k, ny)
        feats = pl.ds(pl.multiple_of(p * part, part), part)
        total = jnp.zeros((part, pick_ref.shape[1]), F32)
        for c in range(pairs):
            both = jnp.concatenate([row_recv[2 * c, feats, :], row_recv[2 * c + 1, feats, :]], axis=1)
            total += jnp.dot(
                both, pick_ref[2 * c * tile : 2 * (c + 1) * tile, :], preferred_element_type=F32
            )
        y_send[p] = total.astype(BF16)

        @pl.when(p != my_y)
        def _():
            y_copy(k).start()
        return 0

    lax.fori_loop(1, ny + 1, to_tokens, 0)
    y_recv[my_y] = y_send[my_y]
    run(1, ny, lambda k: y_arrival(k).wait())

    def z_copy(k):
        p = lax.rem(my_z + k, nz)
        return pltpu.make_async_remote_copy(
            src_ref=z_send.at[p], dst_ref=z_recv.at[my_z], send_sem=z_ss.at[p],
            recv_sem=z_rs.at[my_z], device_id=(my_y * nz + p, ex), device_id_type=MESH,
        )

    def z_arrival(k):
        p = lax.rem(my_z + k, nz)
        return pltpu.make_async_remote_copy(
            src_ref=z_send.at[p], dst_ref=z_recv.at[p], send_sem=z_ss.at[p],
            recv_sem=z_rs.at[p], device_id=(my_y * nz + p, ex), device_id_type=MESH,
        )

    for i in range(nz):
        rows = slice(i * own, (i + 1) * own)
        total = y_recv[0, rows, :].astype(F32)
        for j in range(1, ny):
            total += y_recv[j, rows, :].astype(F32)
        z_send[i] = total.astype(BF16)
    run(1, nz, lambda k: z_copy(k).start())
    z_recv[my_z] = z_send[my_z]
    run(1, nz, lambda k: z_arrival(k).wait())
    total = z_recv[0].astype(F32)
    for j in range(1, nz):
        total += z_recv[j].astype(F32)
    tok_ref[...] = total.astype(BF16)

    run(1, experts, lambda k: se_arrival(k).wait())
    squares = sq_ex[0]
    for j in range(1, experts):
        squares += sq_ex[j]
    squares = jnp.sum(squares, axis=(0, 1), keepdims=True)
    scale = limit / jnp.maximum(jnp.sqrt(squares), limit)

    def clip(src, p):
        cols = pl.ds(pl.multiple_of(p * units, units), units)
        for m in range(3):
            clip_ref[m, :, cols] = (src[p, m].astype(F32) * scale).astype(BF16)

    clip(grad_send, dp)

    def finish(k):
        p = lax.rem(dp + shards - k, shards)
        grad_arrival(p).wait()
        clip(grad_recv, p)

    run(1, shards, finish)


def per_device(sizes, tokens, cotangent, routes, gate_values, gate_weight, up_weight, down_weight):
    experts = lax.axis_size("expert")
    shards = lax.axis_size("dp")
    ny, nz = sizes
    block, width = tokens.shape
    units = gate_weight.shape[2]
    slots = experts * CAP
    own = width // shards

    first, second = slot_match(routes, experts)
    pick = (first | second).astype(BF16)
    gains = jnp.where(
        first, gate_values[:, 0][None, :],
        jnp.where(second, gate_values[:, 1][None, :], jnp.zeros((), BF16)),
    )
    input_send = jnp.dot(pick, tokens, preferred_element_type=F32).astype(BF16)
    weighted_send = jnp.dot(gains, cotangent, preferred_element_type=F32).astype(BF16)
    input_rows = lax.all_to_all(
        input_send.reshape(experts, CAP, width), "expert", split_axis=0, concat_axis=0, tiled=True
    ).reshape(slots, width)
    weighted_rows = lax.all_to_all(
        weighted_send.reshape(experts, CAP, width), "expert", split_axis=0, concat_axis=0, tiled=True
    ).reshape(slots, width)

    limit = CLIP_RMS * math.sqrt(3.0 * experts * width * units * shards)
    vmem = pl.BlockSpec(memory_space=pltpu.VMEM)
    dma = pltpu.SemaphoreType.DMA
    clipped, d_tokens = pl.pallas_call(
        functools.partial(kernel, (ny, nz, experts, limit)),
        out_shape=(
            jax.ShapeDtypeStruct((3, own, units * shards), BF16),
            jax.ShapeDtypeStruct((own, block), BF16),
        ),
        in_specs=[vmem] * 6,
        out_specs=(vmem, vmem),
        scratch_shapes=[
            pltpu.VMEM((slots, units), BF16),
            pltpu.VMEM((slots, 2 * units), BF16),
            pltpu.VMEM((experts, width, CAP), BF16),
            pltpu.VMEM((experts, width, CAP), BF16),
            pltpu.VMEM((shards, 3, own, units), BF16),
            pltpu.VMEM((shards, 3, own, units), BF16),
            pltpu.VMEM((ny, width // ny, block), BF16),
            pltpu.VMEM((ny, width // ny, block), BF16),
            pltpu.VMEM((nz, own, block), BF16),
            pltpu.VMEM((nz, own, block), BF16),
            pltpu.VMEM((8, units), F32),
            pltpu.VMEM((shards, 8, units), F32),
            pltpu.VMEM((experts, 8, units), F32),
            dma((experts,)), dma((experts,)), dma((shards,)), dma((shards,)),
            dma((ny,)), dma((ny,)), dma((nz,)), dma((nz,)),
            dma((shards,)), dma((shards,)), dma((experts,)), dma((experts,)),
        ],
        compiler_params=pltpu.CompilerParams(
            collective_id=0, has_side_effects=True, vmem_limit_bytes=61 * 1024 * 1024
        ),
        cost_estimate=pl.CostEstimate(
            flops=16 * slots * width * units, bytes_accessed=30_000_000, transcendentals=slots * units
        ),
    )(input_rows, weighted_rows, gate_weight[0], up_weight[0], down_weight[0], pick)
    return clipped[None], d_tokens


def solution(mesh):
    nz = 8 if mesh.shape["dp"] % 8 == 0 else mesh.shape["dp"]
    return jax.shard_map(
        functools.partial(per_device, (mesh.shape["dp"] // nz, nz)),
        mesh=mesh,
        in_specs=(
            P("expert", None),
            P("expert", None),
            P("expert", None),
            P("expert", None),
            P("expert", None, "dp"),
            P("expert", None, "dp"),
            P("expert", None, "dp"),
        ),
        out_specs=(P("expert", None, "dp", None), P("dp", "expert")),
        check_vma=False,
    )
```

time: 575 us -> 353 us (0.61)
  blocking collectives: 264 us -> 0 us
  Pallas kernels: 0 us -> 188 us
  local copies, waits for them, and re-layouts: 88.9 us -> 7.74 us
  matrix products: 39 us -> 9.13 us
  other arithmetic: 30.7 us -> 1.72 us
  waiting for transfers between devices: 117 us -> 133 us
  between operations: 15 us -> 0.7 us
    all_to_all x1 -> x0, blocking collectives: 189 us -> none  [per_device(): lax.all_to_all(gradients, 'dp', split_axis=1, concat_axis=2, tiled=True)]
    pallas_call x0 -> x1, Pallas kernels: none -> 188 us  [per_device(): pl.pallas_call(functools.partial(kernel, (ny, nz, experts, limit)), out_s...]
    psum x1 -> x0, blocking collectives: 74.6 us -> none  [per_device(): lax.psum(jnp.sum(jnp.square(owned_rows.astype(jnp.float32))), ('dp', 'exp...]
    dot_general x8 -> x3, matrix products: 39 us -> 9.13 us  [the longest x1 4.47 us: per_device(): jnp.dot(gains, cotangent, preferred_element_type=F32).astype(BF16)]
    gather x4 -> x0, local copies, waits for them, and re-layouts: 28.5 us -> none  [the longest x1 13.8 us: fill_rows(): token_block[token_of_slot]]
    another operation x2 -> x0, local copies, waits for them, and re-layouts: 23.9 us -> none  [the longest x1 23.9 us: expert_pass(): jnp.stack([row_contract(input_rows, grad_gate), row_contract(input_rows,...]
    all_to_all x3 -> x2, waiting for transfers between devices: 110 us -> 133 us  [the longest x1 68 us: per_device(): lax.all_to_all(input_send.reshape(experts, CAP, width), 'expert', split_a...]
    convert_element_type x2, local copies, waits for them, and re-layouts: 13.9 us -> 0.21 us  [slot_match(): position = jnp.sum(jnp.where(onehot, before, 0.0), axis=1).astype(jnp.int32)]
  transfers between devices with their start and end apart: 4 -> 2, of which waited for: 3 -> 2; matrix products, arithmetic and copies ran while one was open for 16% -> 2% of each run, Pallas kernels for 0% -> 0%
where the time goes in v1:
time: 353 us
  Pallas kernels  188 us (53%)
  waiting for transfers between devices  133 us (38%)
  starting transfers between devices  13.1 us (4%)
  matrix products  9.13 us (3%)
  local copies, waits for them, and re-layouts  7.74 us (2%)
    pallas_call x1, Pallas kernels, per_device(): pl.pallas_call(functools.partial(kernel, (ny, nz, experts, limit)), out_s...  188 us
    all_to_all x1, waiting for transfers between devices, per_device(): lax.all_to_all(input_send.reshape(experts, CAP, width), 'expert', split_a...  68 us
    all_to_all x1, waiting for transfers between devices, per_device(): lax.all_to_all(weighted_send.reshape(experts, CAP, width), 'expert', spli...  64.7 us
    all_to_all x1, starting transfers between devices, per_device(): lax.all_to_all(input_send.reshape(experts, CAP, width), 'expert', split_a...  7.83 us
  transfers between devices with their start and end apart: 2, of which 2 were waited for; matrix products, arithmetic and copies ran while one was open for 2% of the time, Pallas kernels for 0%

profile of v1, /device:TPU:12, one launch (start us, length us, event | category | flops | bytes accessed | tf_op | source)
XLA Modules:
  0.0 353.0 jit_solution(6116701640698546222)
XLA Ops:
  0.6 0.0 copy-start
  0.6 0.9 copy.15
  1.6 0.1 eq.46
  1.7 0.3 fusion
  2.0 0.1 convert_element_type.19
  2.2 0.1 copy.16
  2.2 0.7 multiply_add_fusion
  2.9 0.8 slice_reduce_fusion.1
  3.7 0.0 copy-done
  3.7 4.5 %convolution_convert_fusion = bf16[1024,3072]{1,0:T(8,128)(2,1)} fusion(bf16[256,3072]{1,0:T(8,128)(2,1)S(1)} %copy-done, s32[256]{0:T(256)S(1)} %bitcast.18, s32[256]{0:T(256)S(1)} %bitcast.15, bf16[256]{0:T(256)(128)(2,1)S(1)} %get-tuple-element.7, bf16[256]{0:T(256)(128)(2,1)S(1)} %get-tuple-element.6), kind=kOutput, calls=%fused_computation | convolution fusion | flops 1614807040 | bytes 7867392 | tf_op jit(solution)/shard_map/dot_general | solution.py:324
  8.2 0.0 copy-start.1
  8.2 5.3 %all-to-all-start.1 = ((bf16[8,128,3072]{2,1,0:T(8,128)(2,1)}), bf16[8,128,3072]{2,1,0:T(8,128)(2,1)}, u32[]{:S(2)}, u32[]{:S(2)}) async-start(bf16[8,128,3072]{2,1,0:T(8,128)(2,1)} %bitcast.12), calls=%async_computation.1 | async-start | bytes 12582912 | tf_op jit(solution)/shard_map/all_to_all | solution.py:328
  13.5 0.0 copy-done.1
  13.5 4.4 %convolution_convert_fusion.1 = bf16[1024,3072]{1,0:T(8,128)(2,1)} fusion(bf16[256,3072]{1,0:T(8,128)(2,1)S(1)} %copy-done.1, s32[256]{0:T(256)S(1)} %bitcast.19, s32[256]{0:T(256)S(1)} %bitcast.16), kind=kOutput, calls=%fused_computation.1 | convolution fusion | flops 1614544896 | bytes 7866368 | tf_op jit(solution)/shard_map/dot_general | solution.py:323
  17.9 64.7 %all-to-all-done.1 = bf16[8,128,3072]{2,1,0:T(8,128)(2,1)} async-done(((bf16[8,128,3072]{2,1,0:T(8,128)(2,1)}), bf16[8,128,3072]{2,1,0:T(8,128)(2,1)}, u32[]{:S(2)}, u32[]{:S(2)}) %all-to-all-start.1) | async-done | bytes 6291488 | tf_op jit(solution)/shard_map/all_to_all | solution.py:328
  82.5 7.8 %all-to-all-start = ((bf16[8,128,3072]{2,1,0:T(8,128)(2,1)}), bf16[8,128,3072]{2,1,0:T(8,128)(2,1)}, u32[]{:S(2)}, u32[]{:S(2)}) async-start(bf16[8,128,3072]{2,1,0:T(8,128)(2,1)} %bitcast.13), calls=%async_computation | async-start | bytes 12582912 | tf_op jit(solution)/shard_map/all_to_all | solution.py:325
  90.4 1.0 fusion.4.pick_ref
  91.4 68.0 %all-to-all-done = bf16[8,128,3072]{2,1,0:T(8,128)(2,1)} async-done(((bf16[8,128,3072]{2,1,0:T(8,128)(2,1)}), bf16[8,128,3072]{2,1,0:T(8,128)(2,1)}, u32[]{:S(2)}, u32[]{:S(2)}) %all-to-all-start) | async-done | bytes 6291488 | tf_op jit(solution)/shard_map/all_to_all | solution.py:325
  159.4 187.9 %shard_map.86 = (bf16[3,96,8192]{2,1,0:T(8,128)(2,1)}, bf16[96,256]{1,0:T(8,128)(2,1)}) custom-call(bf16[1024,3072]{1,0:T(8,128)(2,1)} %bitcast.3.x_ref, bf16[1024,3072]{1,0:T(8,128)(2,1)} %bitcast.5.w_ref, bf16[3072,256]{1,0:T(8,128)(2,1)} %bitcast.21, bf16[3072,256]{1,0:T(8,128)(2,1)} %bitcast.22, bf16[3072,256]{1,0:T(8,128)(2,1)} %bitcast.23, ...), custom_call_target="tpu_custom_call" | custom-call | flops 12884901888 | bytes 30000000 | tf_op jit(solution)/shard_map/pallas_call | solution.py:335
  347.3 0.0 copy-start.2
  347.3 5.0 %copy.19 = bf16[1,3,96,8192]{3,2,1,0:T(8,128)(2,1)} copy(bf16[1,3,96,8192]{3,2,1,0:T(8,128)(2,1)} %bitcast.14) | data formatting | bytes 9437184
  352.4 0.0 copy-done.2
  352.4 0.6 copy.20
  (2 shorter events, 0.0 us)
Async XLA Ops:
  0.6 3.1 copy-start
  8.2 5.3 %copy-start.1 = (bf16[256,3072]{1,0:T(8,128)(2,1)S(1)}, bf16[256,3072]{1,0:T(8,128)(2,1)}, u32[]{:S(2)}) copy-start(bf16[256,3072]{1,0:T(8,128)(2,1)} %param.7) | copy-start | bytes 4718596
  8.2 74.3 %all-to-all-start.1 = ((bf16[8,128,3072]{2,1,0:T(8,128)(2,1)}), bf16[8,128,3072]{2,1,0:T(8,128)(2,1)}, u32[]{:S(2)}, u32[]{:S(2)}) async-start(bf16[8,128,3072]{2,1,0:T(8,128)(2,1)} %bitcast.12), calls=%async_computation.1 | async-start | bytes 12582912 | tf_op jit(solution)/shard_map/all_to_all | solution.py:328
  82.5 76.9 %all-to-all-start = ((bf16[8,128,3072]{2,1,0:T(8,128)(2,1)}), bf16[8,128,3072]{2,1,0:T(8,128)(2,1)}, u32[]{:S(2)}, u32[]{:S(2)}) async-start(bf16[8,128,3072]{2,1,0:T(8,128)(2,1)} %bitcast.13), calls=%async_computation | async-start | bytes 12582912 | tf_op jit(solution)/shard_map/all_to_all | solution.py:325
  347.3 5.1 %copy-start.2 = (bf16[96,256]{1,0:T(8,128)(2,1)S(1)}, bf16[96,256]{1,0:T(8,128)(2,1)}, u32[]{:S(2)}) copy-start(bf16[96,256]{1,0:T(8,128)(2,1)} %get-tuple-element.13) | copy-start | bytes 147460

commit v2 on v1

--- a/solution.py
+++ b/solution.py
@@ -10,6 +10,7 @@
 
 CAP = 128
 CLIP_RMS = 0.2
+DIRECT = 1280
 MESH = pl.DeviceIdType.MESH
 F32 = jnp.float32
 BF16 = jnp.bfloat16
@@ -29,10 +30,11 @@
 
 def kernel(
     shape,
-    x_ref, w_ref, gate_ref, up_ref, down_ref, pick_ref,
+    tok_in, cot_in, pick_ref, gain_ref, gate_ref, up_ref, down_ref,
     clip_ref, tok_ref,
-    h_ref, g_ref, row_send, row_recv, grad_send, grad_recv,
+    xw_ref, piece_send, direct_send, h_ref, g_ref, row_send, row_recv, grad_send, grad_recv,
     y_send, y_recv, z_send, z_recv, sq_ref, sq_dp, sq_ex,
+    piece_ss, piece_rs, direct_ss, direct_rs, za_ss, za_rs, ya_ss, ya_rs, out_sem,
     row_ss, row_rs, grad_ss, grad_rs, y_ss, y_rs, z_ss, z_rs, sd_ss, sd_rs, se_ss, se_rs,
 ):
     ny, nz, experts, limit = shape
@@ -40,7 +42,8 @@
     dp = lax.axis_index("dp")
     ex = lax.axis_index("expert")
     my_y, my_z = dp // nz, lax.rem(dp, nz)
-    slots, width = x_ref.shape
+    slots = pick_ref.shape[0]
+    width = tok_in.shape[1]
     units = gate_ref.shape[1]
     own = width // shards
     group = own * 4
@@ -65,13 +68,137 @@
     lax.fori_loop(1, experts, greet_ex, 0)
     pl.semaphore_wait(barrier, shards + experts - 2)
 
-    chunk = 256
+    def run(first, count, do):
+        def body(k, _):
+            do(k)
+            return 0
+        lax.fori_loop(first, count, body, 0)
+
+    direct = direct_send.shape[-1]
+    half = (width - direct) // 2
+    rows16 = tile // nz
+    my_array, my_half = my_y // 2, lax.rem(my_y, 2)
+
+    def cols_of(q):
+        return pl.ds(pl.multiple_of(direct + lax.rem(q, 2) * half, 128), half)
+
+    def rows_of(z):
+        return pl.ds(pl.multiple_of(z * rows16, rows16), rows16)
+
+    def make_piece(select_ref, values_ref):
+        picked = jnp.concatenate(
+            [
+                select_ref[pl.ds(pl.multiple_of(e * tile + my_z * rows16, rows16), rows16), :]
+                for e in range(experts)
+            ],
+            axis=0,
+        )
+        made = jnp.dot(picked, values_ref[:, cols_of(my_y)], preferred_element_type=F32).astype(BF16)
+        for e in range(experts):
+            piece_send[e] = made[e * rows16 : (e + 1) * rows16]
+
+    @pl.when(my_array == 0)
+    def _():
+        make_piece(pick_ref, tok_in)
+
+    @pl.when(my_array == 1)
+    def _():
+        make_piece(gain_ref, cot_in)
+
+    def piece_copy(e, b):
+        return pltpu.make_async_remote_copy(
+            src_ref=piece_send.at[e], dst_ref=xw_ref.at[my_array, b, rows_of(my_z), cols_of(my_y)],
+            send_sem=piece_ss.at[e], recv_sem=piece_rs.at[b], device_id=(dp, e), device_id_type=MESH,
+        )
+
+    run(1, experts, lambda k: piece_copy(lax.rem(ex + k, experts), ex).start())
+    xw_ref[my_array, ex, rows_of(my_z), cols_of(my_y)] = piece_send[ex]
+
+    def direct_copy(e, b):
+        return pltpu.make_async_remote_copy(
+            src_ref=direct_send.at[e], dst_ref=xw_ref.at[:, b, :, pl.ds(0, direct)],
+            send_sem=direct_ss.at[e], recv_sem=direct_rs.at[b], device_id=(dp, e), device_id_type=MESH,
+        )
+
+    def make_direct(k, _):
+        e = lax.rem(ex + k, experts)
+        rows = pl.ds(pl.multiple_of(e * tile, tile), tile)
+        for m, (select_ref, values_ref) in enumerate(((pick_ref, tok_in), (gain_ref, cot_in))):
+            direct_send[e, m] = jnp.dot(
+                select_ref[rows, :], values_ref[:, :direct], preferred_element_type=F32
+            ).astype(BF16)
+
+        @pl.when(e != ex)
+        def _():
+            direct_copy(e, ex).start()
+        return 0
+
+    lax.fori_loop(1, experts + 1, make_direct, 0)
+    xw_ref[:, ex, :, :direct] = direct_send[ex]
+
+    def wait_piece(k):
+        e = lax.rem(ex + k, experts)
+        piece_copy(e, e).wait()
+
+    run(1, experts, wait_piece)
+
+    def z_of(k):
+        return lax.rem(my_z + (nz - (k + 1) // 2 if k % 2 else k // 2), nz)
+
+    def z_step(k, source):
+        piece = xw_ref.at[my_array, :, rows_of(source), cols_of(my_y)]
+        to = lax.rem(my_z + (1 if k % 2 else nz - 1), nz)
+        return pltpu.make_async_remote_copy(
+            src_ref=piece, dst_ref=piece, send_sem=za_ss.at[k], recv_sem=za_rs.at[k],
+            device_id=(my_y * nz + to, ex), device_id_type=MESH,
+        )
+
+    def y_step(k, q, way, index):
+        piece = xw_ref.at[q // 2, :, rows_of(z_of(k)), cols_of(q)]
+        to = lax.rem(my_y + way, ny)
+        return pltpu.make_async_remote_copy(
+            src_ref=piece, dst_ref=piece, send_sem=ya_ss.at[k, index], recv_sem=ya_rs.at[k, index],
+            device_id=(to * nz + my_z, ex), device_id_type=MESH,
+        )
+
+    up_q, down_q, far_q = lax.rem(my_y + 1, ny), lax.rem(my_y + ny - 1, ny), lax.rem(my_y + 2, ny)
+
+    def y_forward(k):
+        y_step(k, down_q, 1, 0).wait_recv()
+        y_step(k, up_q, ny - 1, 1).wait_recv()
+        if k % 2:
+            y_step(k, up_q, ny - 1, 2).start()
+        else:
+            y_step(k, down_q, 1, 2).start()
+
+    for k in range(nz):
+        if k:
+            z_step(k, z_of(k)).wait_recv()
+        for later in ((1, 2) if k == 0 else (k + 2,)):
+            if later < nz:
+                z_step(later, z_of(k)).start()
+        y_step(k, my_y, 1, 0).start()
+        y_step(k, my_y, ny - 1, 1).start()
+        if k >= 2:
+            y_forward(k - 2)
+    y_forward(nz - 2)
+    y_forward(nz - 1)
+    for k in range(nz):
+        y_step(k, far_q, 1, 2).wait_recv()
+
+    def wait_direct(k):
+        e = lax.rem(ex + k, experts)
+        direct_copy(e, e).wait()
+
+    run(1, experts, wait_direct)
 
     def hidden(i, _):
-        rows = pl.ds(pl.multiple_of(i * chunk, chunk), chunk)
-        pre_gate = jnp.dot(x_ref[rows, :], gate_ref[...], preferred_element_type=F32)
-        pre_up = jnp.dot(x_ref[rows, :], up_ref[...], preferred_element_type=F32)
-        grad_hidden = jnp.dot(w_ref[rows, :], down_ref[...], preferred_element_type=F32)
+        rows = pl.ds(pl.multiple_of(i * 2 * tile, 2 * tile), 2 * tile)
+        x = xw_ref[0, pl.ds(2 * i, 2)].reshape(2 * tile, width)
+        w = xw_ref[1, pl.ds(2 * i, 2)].reshape(2 * tile, width)
+        pre_gate = jnp.dot(x, gate_ref[...], preferred_element_type=F32)
+        pre_up = jnp.dot(x, up_ref[...], preferred_element_type=F32)
+        grad_hidden = jnp.dot(w, down_ref[...], preferred_element_type=F32)
         s = jax.nn.sigmoid(pre_gate)
         act = pre_gate * s
         h_ref[rows, :] = (act * pre_up).astype(BF16)
@@ -81,7 +208,13 @@
         g_ref[rows, units:] = (grad_hidden * act).astype(BF16)
         return 0
 
-    lax.fori_loop(0, slots // chunk, hidden, 0)
+    lax.fori_loop(0, experts // 2, hidden, 0)
+
+    for k in range(nz):
+        if k:
+            z_step(k, z_of(k)).wait_send()
+        for index in range(3):
+            y_step(k, my_y, 1, index).wait_send()
 
     def row_copy(e):
         return pltpu.make_async_remote_copy(
@@ -149,10 +282,10 @@
         feats = pl.ds(pl.multiple_of(c * group, group), group)
         total = jnp.zeros(sq_ref.shape, F32)
         first = lax.dot_general(
-            x_ref[:, feats], g_ref[...], (((0,), (0,)), ((), ())), preferred_element_type=F32
+            xw_ref[0, :, :, feats].reshape(slots, group), g_ref[...], (((0,), (0,)), ((), ())), preferred_element_type=F32
         ).astype(BF16)
         last = lax.dot_general(
-            w_ref[:, feats], h_ref[...], (((0,), (0,)), ((), ())), preferred_element_type=F32
+            xw_ref[1, :, :, feats].reshape(slots, group), h_ref[...], (((0,), (0,)), ((), ())), preferred_element_type=F32
         ).astype(BF16)
         for i in range(4):
             rows = slice(i * own, (i + 1) * own)
@@ -198,12 +331,6 @@
             recv_sem=se_rs.at[p], device_id=(dp, p), device_id_type=MESH,
         )
 
-    def run(first, count, do):
-        def body(k, _):
-            do(k)
-            return 0
-        lax.fori_loop(first, count, body, 0)
-
     run(1, shards, lambda k: sd_copy(k).start())
     run(1, shards, lambda k: sd_arrival(k).wait())
 
@@ -290,10 +417,17 @@
     squares = jnp.sum(squares, axis=(0, 1), keepdims=True)
     scale = limit / jnp.maximum(jnp.sqrt(squares), limit)
 
+    def out_copy(p):
+        return pltpu.make_async_copy(
+            grad_send.at[p],
+            clip_ref.at[:, :, pl.ds(pl.multiple_of(p * units, units), units)],
+            out_sem.at[p],
+        )
+
     def clip(src, p):
-        cols = pl.ds(pl.multiple_of(p * units, units), units)
         for m in range(3):
-            clip_ref[m, :, cols] = (src[p, m].astype(F32) * scale).astype(BF16)
+            grad_send[p, m] = (src[p, m].astype(F32) * scale).astype(BF16)
+        out_copy(p).start()
 
     clip(grad_send, dp)
 
@@ -303,6 +437,7 @@
         clip(grad_recv, p)
 
     run(1, shards, finish)
+    run(0, shards, lambda k: out_copy(k).wait())
 
 
 def per_device(sizes, tokens, cotangent, routes, gate_values, gate_weight, up_weight, down_weight):
@@ -320,15 +455,6 @@
         first, gate_values[:, 0][None, :],
         jnp.where(second, gate_values[:, 1][None, :], jnp.zeros((), BF16)),
     )
-    input_send = jnp.dot(pick, tokens, preferred_element_type=F32).astype(BF16)
-    weighted_send = jnp.dot(gains, cotangent, preferred_element_type=F32).astype(BF16)
-    input_rows = lax.all_to_all(
-        input_send.reshape(experts, CAP, width), "expert", split_axis=0, concat_axis=0, tiled=True
-    ).reshape(slots, width)
-    weighted_rows = lax.all_to_all(
-        weighted_send.reshape(experts, CAP, width), "expert", split_axis=0, concat_axis=0, tiled=True
-    ).reshape(slots, width)
-
     limit = CLIP_RMS * math.sqrt(3.0 * experts * width * units * shards)
     vmem = pl.BlockSpec(memory_space=pltpu.VMEM)
     dma = pltpu.SemaphoreType.DMA
@@ -338,9 +464,12 @@
             jax.ShapeDtypeStruct((3, own, units * shards), BF16),
             jax.ShapeDtypeStruct((own, block), BF16),
         ),
-        in_specs=[vmem] * 6,
-        out_specs=(vmem, vmem),
+        in_specs=[vmem] * 7,
+        out_specs=(pl.BlockSpec(memory_space=pl.ANY), vmem),
         scratch_shapes=[
+            pltpu.VMEM((2, experts, CAP, width), BF16),
+            pltpu.VMEM((experts, CAP // nz, (width - DIRECT) // 2), BF16),
+            pltpu.VMEM((experts, 2, CAP, DIRECT), BF16),
             pltpu.VMEM((slots, units), BF16),
             pltpu.VMEM((slots, 2 * units), BF16),
             pltpu.VMEM((experts, width, CAP), BF16),
@@ -354,6 +483,8 @@
             pltpu.VMEM((8, units), F32),
             pltpu.VMEM((shards, 8, units), F32),
             pltpu.VMEM((experts, 8, units), F32),
+            dma((experts,)), dma((experts,)), dma((experts,)), dma((experts,)),
+            dma((nz,)), dma((nz,)), dma((nz, 3)), dma((nz, 3)), dma((shards,)),
             dma((experts,)), dma((experts,)), dma((shards,)), dma((shards,)),
             dma((ny,)), dma((ny,)), dma((nz,)), dma((nz,)),
             dma((shards,)), dma((shards,)), dma((experts,)), dma((experts,)),
@@ -364,7 +495,7 @@
         cost_estimate=pl.CostEstimate(
             flops=16 * slots * width * units, bytes_accessed=30_000_000, transcendentals=slots * units
         ),
-    )(input_rows, weighted_rows, gate_weight[0], up_weight[0], down_weight[0], pick)
+    )(tokens, cotangent, pick, gains, gate_weight[0], up_weight[0], down_weight[0])
     return clipped[None], d_tokens
 
 

time: 353 us -> 260 us (0.74)
  waiting for transfers between devices: 133 us -> 0 us
  Pallas kernels: 188 us -> 247 us
  starting transfers between devices: 13.1 us -> 0 us
  matrix products: 9.13 us -> 0.26 us
    all_to_all x2 -> x0, waiting for transfers between devices: 133 us -> none  [the longest x1 68 us: per_device(): lax.all_to_all(input_send.reshape(experts, CAP, width), 'expert', split_a...]
    pallas_call x1, Pallas kernels: 188 us -> 247 us  [per_device(): pl.pallas_call(functools.partial(kernel, (ny, nz, experts, limit)), out_s...]
    all_to_all x2 -> x0, starting transfers between devices: 13.1 us -> none  [the longest x1 7.83 us: per_device(): lax.all_to_all(input_send.reshape(experts, CAP, width), 'expert', split_a...]
    dot_general x2 -> x0, matrix products: 8.87 us -> none  [the longest x1 4.47 us: per_device(): jnp.dot(gains, cotangent, preferred_element_type=F32).astype(BF16)]
  transfers between devices with their start and end apart: 2 -> 0, of which waited for: 2 -> 0; matrix products, arithmetic and copies ran while one was open for 2% -> 0% of each run, Pallas kernels for 0% -> 0%
where the time goes in v2:
time: 260 us; the launch traced here: 258 us
  Pallas kernels  247 us (95%)
  local copies, waits for them, and re-layouts  7.61 us (3%)
  other arithmetic  2.75 us (1%)
    pallas_call x1, Pallas kernels, per_device(): pl.pallas_call(functools.partial(kernel, (ny, nz, experts, limit)), out_s...  247 us
    unnamed x5, local copies, waits for them, and re-layouts  6.47 us

profile of v2, /device:TPU:12, one launch (start us, length us, event | category | flops | bytes accessed | tf_op | source)
XLA Modules:
  0.0 258.4 jit_solution(9723060228567602474)
XLA Ops:
  0.6 0.8 slice_reduce_fusion.1
  1.4 0.8 copy.15
  2.2 0.1 eq.46
  2.4 0.3 fusion
  2.6 0.1 convert_element_type.13
  2.8 0.1 copy.16
  2.9 0.7 multiply_add_fusion
  3.6 1.0 fusion.3.gain_ref
  4.6 1.0 fusion.4.pick_ref
  5.6 247.1 %shard_map.86 = (bf16[3,96,8192]{2,1,0:T(8,128)(2,1)}, bf16[96,256]{1,0:T(8,128)(2,1)}) custom-call(bf16[256,3072]{1,0:T(8,128)(2,1)} %tok_in.1, bf16[256,3072]{1,0:T(8,128)(2,1)} %cot_in.1, bf16[1024,256]{1,0:T(8,128)(2,1)} %fusion.4.pick_ref, bf16[1024,256]{1,0:T(8,128)(2,1)} %fusion.3.gain_ref, bf16[3072,256]{1,0:T(8,128)(2,1)} %bitcast.11, ...), custom_call_target="tpu_custom_call" | custom-call | flops 12884901888 | bytes 30000000 | tf_op jit(solution)/shard_map/pallas_call | solution.py:461
  252.8 0.0 copy-start
  252.8 5.0 %copy.19 = bf16[1,3,96,8192]{3,2,1,0:T(8,128)(2,1)} copy(bf16[1,3,96,8192]{3,2,1,0:T(8,128)(2,1)} %bitcast.6) | data formatting | bytes 9437184
  257.8 0.0 copy-done
  257.8 0.6 copy.20
  (2 shorter events, 0.0 us)
Async XLA Ops:
  252.8 5.1 %copy-start = (bf16[96,256]{1,0:T(8,128)(2,1)S(1)}, bf16[96,256]{1,0:T(8,128)(2,1)}, u32[]{:S(2)}) copy-start(bf16[96,256]{1,0:T(8,128)(2,1)} %get-tuple-element.13) | copy-start | bytes 147460

commit v3 on v2

--- a/solution.py
+++ b/solution.py
@@ -10,7 +10,8 @@
 
 CAP = 128
 CLIP_RMS = 0.2
-DIRECT = 1280
+DIRECT = 1024
+BAND = 640
 MESH = pl.DeviceIdType.MESH
 F32 = jnp.float32
 BF16 = jnp.bfloat16
@@ -34,7 +35,7 @@
     clip_ref, tok_ref,
     xw_ref, piece_send, direct_send, h_ref, g_ref, row_send, row_recv, grad_send, grad_recv,
     y_send, y_recv, z_send, z_recv, sq_ref, sq_dp, sq_ex,
-    piece_ss, piece_rs, direct_ss, direct_rs, za_ss, za_rs, ya_ss, ya_rs, out_sem,
+    piece_ss, piece_rs, direct_ss, direct_rs, za_ss, za_rs, ya_ss, ya_rs, yb_ss, yb_rs, zb_ss, zb_rs, out_sem,
     row_ss, row_rs, grad_ss, grad_rs, y_ss, y_rs, z_ss, z_rs, sd_ss, sd_rs, se_ss, se_rs,
 ):
     ny, nz, experts, limit = shape
@@ -75,12 +76,16 @@
         lax.fori_loop(first, count, body, 0)
 
     direct = direct_send.shape[-1]
-    half = (width - direct) // 2
+    half, late = BAND, (width - direct) // 2 - BAND
+    late_from = direct + 2 * half
     rows16 = tile // nz
     my_array, my_half = my_y // 2, lax.rem(my_y, 2)
 
     def cols_of(q):
         return pl.ds(pl.multiple_of(direct + lax.rem(q, 2) * half, 128), half)
+
+    def late_of(q):
+        return pl.ds(pl.multiple_of(late_from + lax.rem(q, 2) * late, 128), late)
 
     def rows_of(z):
         return pl.ds(pl.multiple_of(z * rows16, rows16), rows16)
@@ -93,9 +98,10 @@
             ],
             axis=0,
         )
-        made = jnp.dot(picked, values_ref[:, cols_of(my_y)], preferred_element_type=F32).astype(BF16)
-        for e in range(experts):
-            piece_send[e] = made[e * rows16 : (e + 1) * rows16]
+        for cols, to in ((cols_of(my_y), slice(0, half)), (late_of(my_y), slice(half, half + late))):
+            made = jnp.dot(picked, values_ref[:, cols], preferred_element_type=F32).astype(BF16)
+            for e in range(experts):
+                piece_send[e, :, to] = made[e * rows16 : (e + 1) * rows16]
 
     @pl.when(my_array == 0)
     def _():
@@ -105,14 +111,22 @@
     def _():
         make_piece(gain_ref, cot_in)
 
-    def piece_copy(e, b):
-        return pltpu.make_async_remote_copy(
-            src_ref=piece_send.at[e], dst_ref=xw_ref.at[my_array, b, rows_of(my_z), cols_of(my_y)],
-            send_sem=piece_ss.at[e], recv_sem=piece_rs.at[b], device_id=(dp, e), device_id_type=MESH,
-        )
-
-    run(1, experts, lambda k: piece_copy(lax.rem(ex + k, experts), ex).start())
-    xw_ref[my_array, ex, rows_of(my_z), cols_of(my_y)] = piece_send[ex]
+    def piece_copy(e, b, m):
+        cols = cols_of(my_y) if m == 0 else late_of(my_y)
+        return pltpu.make_async_remote_copy(
+            src_ref=piece_send.at[e, :, pl.ds(0, half) if m == 0 else pl.ds(half, late)],
+            dst_ref=xw_ref.at[my_array, b, rows_of(my_z), cols],
+            send_sem=piece_ss.at[m, e], recv_sem=piece_rs.at[m, b],
+            device_id=(dp, e), device_id_type=MESH,
+        )
+
+    def send_piece(k):
+        for m in (1, 0):
+            piece_copy(lax.rem(ex + k, experts), ex, m).start()
+
+    run(1, experts, send_piece)
+    xw_ref[my_array, ex, rows_of(my_z), cols_of(my_y)] = piece_send[ex, :, :half]
+    xw_ref[my_array, ex, rows_of(my_z), late_of(my_y)] = piece_send[ex, :, half:]
 
     def direct_copy(e, b):
         return pltpu.make_async_remote_copy(
@@ -138,30 +152,35 @@
 
     def wait_piece(k):
         e = lax.rem(ex + k, experts)
-        piece_copy(e, e).wait()
+        for m in (1, 0):
+            piece_copy(e, e, m).wait()
 
     run(1, experts, wait_piece)
 
+    def to_y(way):
+        return (lax.rem(my_y + way, ny) * nz + my_z, ex)
+
+    def to_z(way):
+        return (my_y * nz + lax.rem(my_z + way, nz), ex)
+
+    def pass_on(piece, sems, index, device):
+        return pltpu.make_async_remote_copy(
+            src_ref=piece, dst_ref=piece, send_sem=sems[0].at[index], recv_sem=sems[1].at[index],
+            device_id=device, device_id_type=MESH,
+        )
+
+    up_q, down_q, far_q = lax.rem(my_y + 1, ny), lax.rem(my_y + ny - 1, ny), lax.rem(my_y + 2, ny)
+
     def z_of(k):
-        return lax.rem(my_z + (nz - (k + 1) // 2 if k % 2 else k // 2), nz)
+        return lax.rem(my_z + (k // 2 + 1 if k % 2 else nz - k // 2), nz)
 
     def z_step(k, source):
         piece = xw_ref.at[my_array, :, rows_of(source), cols_of(my_y)]
-        to = lax.rem(my_z + (1 if k % 2 else nz - 1), nz)
-        return pltpu.make_async_remote_copy(
-            src_ref=piece, dst_ref=piece, send_sem=za_ss.at[k], recv_sem=za_rs.at[k],
-            device_id=(my_y * nz + to, ex), device_id_type=MESH,
-        )
+        return pass_on(piece, (za_ss, za_rs), k, to_z(nz - 1 if k % 2 else 1))
 
     def y_step(k, q, way, index):
         piece = xw_ref.at[q // 2, :, rows_of(z_of(k)), cols_of(q)]
-        to = lax.rem(my_y + way, ny)
-        return pltpu.make_async_remote_copy(
-            src_ref=piece, dst_ref=piece, send_sem=ya_ss.at[k, index], recv_sem=ya_rs.at[k, index],
-            device_id=(to * nz + my_z, ex), device_id_type=MESH,
-        )
-
-    up_q, down_q, far_q = lax.rem(my_y + 1, ny), lax.rem(my_y + ny - 1, ny), lax.rem(my_y + 2, ny)
+        return pass_on(piece, (ya_ss, ya_rs), 3 * k + index, to_y(way))
 
     def y_forward(k):
         y_step(k, down_q, 1, 0).wait_recv()
@@ -171,7 +190,7 @@
         else:
             y_step(k, down_q, 1, 2).start()
 
-    for k in range(nz):
+    def z_arrive(k):
         if k:
             z_step(k, z_of(k)).wait_recv()
         for later in ((1, 2) if k == 0 else (k + 2,)):
@@ -179,10 +198,54 @@
                 z_step(later, z_of(k)).start()
         y_step(k, my_y, 1, 0).start()
         y_step(k, my_y, ny - 1, 1).start()
-        if k >= 2:
-            y_forward(k - 2)
-    y_forward(nz - 2)
-    y_forward(nz - 1)
+
+    def ly_step(q, way, index):
+        piece = xw_ref.at[q // 2, :, rows_of(my_z), late_of(q)]
+        return pass_on(piece, (yb_ss, yb_rs), index, to_y(way))
+
+    def lz_of(k):
+        return lax.rem(my_z + (nz - (k + 1) // 2 if k % 2 else k // 2), nz)
+
+    def lz_step(k, source):
+        piece = xw_ref.at[:, :, rows_of(source), pl.ds(late_from, 2 * late)]
+        return pass_on(piece, (zb_ss, zb_rs), k, to_z(1 if k % 2 else nz - 1))
+
+    def lz_arrive(k):
+        lz_step(k, lz_of(k)).wait_recv()
+        if k + 2 < nz:
+            lz_step(k + 2, lz_of(k)).start()
+
+    ly_step(my_y, 1, 0).start()
+    ly_step(my_y, ny - 1, 1).start()
+    z_arrive(0)
+    ly_step(down_q, 1, 0).wait_recv()
+    ly_step(down_q, 1, 2).start()
+    ly_step(up_q, ny - 1, 1).wait_recv()
+    z_arrive(1)
+    z_arrive(2)
+    y_forward(0)
+    ly_step(far_q, 1, 2).wait_recv()
+    lz_step(1, my_z).start()
+    lz_step(2, my_z).start()
+    z_arrive(3)
+    z_arrive(4)
+    y_forward(1)
+    z_arrive(5)
+    z_arrive(6)
+    y_forward(2)
+    z_arrive(7)
+    y_forward(3)
+    lz_arrive(1)
+    lz_arrive(2)
+    y_forward(4)
+    y_forward(5)
+    lz_arrive(3)
+    lz_arrive(4)
+    y_forward(6)
+    lz_arrive(5)
+    lz_arrive(6)
+    y_forward(7)
+    lz_arrive(7)
     for k in range(nz):
         y_step(k, far_q, 1, 2).wait_recv()
 
@@ -213,8 +276,11 @@
     for k in range(nz):
         if k:
             z_step(k, z_of(k)).wait_send()
+            lz_step(k, lz_of(k)).wait_send()
         for index in range(3):
             y_step(k, my_y, 1, index).wait_send()
+    for index in range(3):
+        ly_step(my_y, 1, index).wait_send()
 
     def row_copy(e):
         return pltpu.make_async_remote_copy(
@@ -259,8 +325,6 @@
                 row_copy(e0 + i).start()
         return 0
 
-    lax.fori_loop(0, pairs, row_pair, 0)
-
     def grad_copy(p):
         return pltpu.make_async_remote_copy(
             src_ref=grad_send.at[p], dst_ref=grad_recv.at[dp],
@@ -277,8 +341,10 @@
 
     sq_ref[...] = jnp.zeros_like(sq_ref)
 
-    def grad_group(k, _):
-        c = lax.rem(dp // 4 + k, groups)
+    def grad_group(n):
+        m = lax.rem(n, 4)
+        to = lax.rem(my_y + 2 * lax.rem(m, 2) + m // 2, ny)
+        c = 2 * to + lax.rem(my_z // 4 + m + 1 + n // 4, 2)
         feats = pl.ds(pl.multiple_of(c * group, group), group)
         total = jnp.zeros(sq_ref.shape, F32)
         first = lax.dot_general(
@@ -296,12 +362,19 @@
                 total += jnp.sum(wide.reshape(own // 8, 8, units), axis=0)
         sq_ref[...] += total
         for i in range(4):
-            @pl.when(4 * c + i != dp)
+            p = 4 * c + lax.rem(my_z + i, 4)
+
+            @pl.when(p != dp)
             def _():
-                grad_copy(4 * c + i).start()
-        return 0
-
-    lax.fori_loop(0, groups, grad_group, 0)
+                grad_copy(p).start()
+
+    def both_kinds(k, _):
+        row_pair(k, 0)
+        grad_group(2 * k)
+        grad_group(2 * k + 1)
+        return 0
+
+    lax.fori_loop(0, pairs, both_kinds, 0)
 
     def sd_copy(k):
         p = lax.rem(dp + k, shards)
@@ -483,8 +556,9 @@
             pltpu.VMEM((8, units), F32),
             pltpu.VMEM((shards, 8, units), F32),
             pltpu.VMEM((experts, 8, units), F32),
-            dma((experts,)), dma((experts,)), dma((experts,)), dma((experts,)),
-            dma((nz,)), dma((nz,)), dma((nz, 3)), dma((nz, 3)), dma((shards,)),
+            dma((2, experts)), dma((2, experts)), dma((experts,)), dma((experts,)),
+            dma((nz,)), dma((nz,)), dma((3 * nz,)), dma((3 * nz,)),
+            dma((3,)), dma((3,)), dma((nz,)), dma((nz,)), dma((shards,)),
             dma((experts,)), dma((experts,)), dma((shards,)), dma((shards,)),
             dma((ny,)), dma((ny,)), dma((nz,)), dma((nz,)),
             dma((shards,)), dma((shards,)), dma((experts,)), dma((experts,)),

time: 260 us -> 245 us (0.942)
  the two profiles are of different devices: /device:TPU:12 before, /device:TPU:2 now
where the time goes in v3:
time: 245 us
  Pallas kernels  234 us (96%)
  local copies, waits for them, and re-layouts  7.61 us (3%)
  other arithmetic  2.75 us (1%)
    pallas_call x1, Pallas kernels, per_device(): pl.pallas_call(functools.partial(kernel, (ny, nz, experts, limit)), out_s...  234 us
    unnamed x5, local copies, waits for them, and re-layouts  6.47 us

profile of v3, /device:TPU:2, one launch (start us, length us, event | category | flops | bytes accessed | tf_op | source)
XLA Modules:
  0.0 245.3 jit_solution(1090927929576181213)
XLA Ops:
  0.6 0.8 slice_reduce_fusion.1
  1.4 0.8 copy.15
  2.2 0.1 eq.46
  2.4 0.3 fusion
  2.6 0.1 convert_element_type.13
  2.8 0.1 copy.16
  2.9 0.7 multiply_add_fusion
  3.6 1.0 fusion.3.gain_ref
  4.6 1.0 fusion.4.pick_ref
  5.6 234.0 %shard_map.86 = (bf16[3,96,8192]{2,1,0:T(8,128)(2,1)}, bf16[96,256]{1,0:T(8,128)(2,1)}) custom-call(bf16[256,3072]{1,0:T(8,128)(2,1)} %tok_in.1, bf16[256,3072]{1,0:T(8,128)(2,1)} %cot_in.1, bf16[1024,256]{1,0:T(8,128)(2,1)} %fusion.4.pick_ref, bf16[1024,256]{1,0:T(8,128)(2,1)} %fusion.3.gain_ref, bf16[3072,256]{1,0:T(8,128)(2,1)} %bitcast.11, ...), custom_call_target="tpu_custom_call" | custom-call | flops 12884901888 | bytes 30000000 | tf_op jit(solution)/shard_map/pallas_call | solution.py:534
  239.6 0.0 copy-start
  239.6 5.0 %copy.19 = bf16[1,3,96,8192]{3,2,1,0:T(8,128)(2,1)} copy(bf16[1,3,96,8192]{3,2,1,0:T(8,128)(2,1)} %bitcast.6) | data formatting | bytes 9437184
  244.6 0.0 copy-done
  244.6 0.6 copy.20
  (2 shorter events, 0.0 us)
Async XLA Ops:
  239.6 5.1 %copy-start = (bf16[96,256]{1,0:T(8,128)(2,1)S(1)}, bf16[96,256]{1,0:T(8,128)(2,1)}, u32[]{:S(2)}) copy-start(bf16[96,256]{1,0:T(8,128)(2,1)} %get-tuple-element.13) | copy-start | bytes 147460

commit v4 on v3

--- a/solution.py
+++ b/solution.py
@@ -12,28 +12,44 @@
 CLIP_RMS = 0.2
 DIRECT = 1024
 BAND = 640
+EARLY = 7
 MESH = pl.DeviceIdType.MESH
 F32 = jnp.float32
 BF16 = jnp.bfloat16
 
 
-def slot_match(routes, experts):
-    flat = routes.reshape(-1)
-    pairs = flat.shape[0]
-    onehot = flat[:, None] == jnp.arange(experts, dtype=jnp.int32)[None, :]
-    earlier = jnp.arange(pairs)[None, :] < jnp.arange(pairs)[:, None]
-    before = jnp.dot(earlier.astype(BF16), onehot.astype(BF16), preferred_element_type=F32)
-    position = jnp.sum(jnp.where(onehot, before, 0.0), axis=1).astype(jnp.int32)
-    slot = (flat * CAP + position).reshape(routes.shape)
-    slots = jnp.arange(experts * CAP, dtype=jnp.int32)[:, None]
-    return slots == slot[:, 0][None, :], slots == slot[:, 1][None, :]
+def fill_slots(routes_ref, gates_ref, pick_ref, gain_ref, experts):
+    slots, block = pick_ref.shape
+    first, second = routes_ref[0:1, :], routes_ref[1:2, :]
+    expert = lax.broadcasted_iota(jnp.int32, (experts, block), 0)
+    on_first, on_second = expert == first, expert == second
+    named = jnp.where(on_first | on_second, 1.0, 0.0).astype(BF16)
+    token = lax.broadcasted_iota(jnp.int32, (block, block), 0)
+    later = lax.broadcasted_iota(jnp.int32, (block, block), 1)
+    earlier = jnp.where(token < later, 1.0, 0.0).astype(BF16)
+    before = jnp.dot(named, earlier, preferred_element_type=F32)
+
+    def slot_of(choice, on):
+        position = jnp.sum(jnp.where(on, before, 0.0), axis=0, keepdims=True)
+        return choice * CAP + position.astype(jnp.int32)
+
+    slot_first, slot_second = slot_of(first, on_first), slot_of(second, on_second)
+    gate_first, gate_second = gates_ref[0:1, :].astype(F32), gates_ref[1:2, :].astype(F32)
+    for start in range(0, slots, 256):
+        slot = lax.broadcasted_iota(jnp.int32, (256, block), 0) + start
+        is_first, is_second = slot == slot_first, slot == slot_second
+        rows = slice(start, start + 256)
+        pick_ref[rows, :] = jnp.where(is_first | is_second, 1.0, 0.0).astype(BF16)
+        gain_ref[rows, :] = jnp.where(
+            is_first, gate_first, jnp.where(is_second, gate_second, 0.0)
+        ).astype(BF16)
 
 
 def kernel(
     shape,
-    tok_in, cot_in, pick_ref, gain_ref, gate_ref, up_ref, down_ref,
+    tok_in, cot_in, routes_ref, gates_ref, gate_ref, up_ref, down_ref,
     clip_ref, tok_ref,
-    xw_ref, piece_send, direct_send, h_ref, g_ref, row_send, row_recv, grad_send, grad_recv,
+    pick_ref, gain_ref, xw_ref, piece_send, direct_send, h_ref, g_ref, row_send, row_recv, grad_send, grad_recv,
     y_send, y_recv, z_send, z_recv, sq_ref, sq_dp, sq_ex,
     piece_ss, piece_rs, direct_ss, direct_rs, za_ss, za_rs, ya_ss, ya_rs, yb_ss, yb_rs, zb_ss, zb_rs, out_sem,
     row_ss, row_rs, grad_ss, grad_rs, y_ss, y_rs, z_ss, z_rs, sd_ss, sd_rs, se_ss, se_rs,
@@ -67,7 +83,7 @@
 
     lax.fori_loop(1, shards, greet_dp, 0)
     lax.fori_loop(1, experts, greet_ex, 0)
-    pl.semaphore_wait(barrier, shards + experts - 2)
+    fill_slots(routes_ref, gates_ref, pick_ref, gain_ref, experts)
 
     def run(first, count, do):
         def body(k, _):
@@ -110,6 +126,8 @@
     @pl.when(my_array == 1)
     def _():
         make_piece(gain_ref, cot_in)
+
+    pl.semaphore_wait(barrier, shards + experts - 2)
 
     def piece_copy(e, b, m):
         cols = cols_of(my_y) if m == 0 else late_of(my_y)
@@ -206,46 +224,55 @@
     def lz_of(k):
         return lax.rem(my_z + (nz - (k + 1) // 2 if k % 2 else k // 2), nz)
 
-    def lz_step(k, source):
-        piece = xw_ref.at[:, :, rows_of(source), pl.ds(late_from, 2 * late)]
-        return pass_on(piece, (zb_ss, zb_rs), k, to_z(1 if k % 2 else nz - 1))
-
-    def lz_arrive(k):
-        lz_step(k, lz_of(k)).wait_recv()
-        if k + 2 < nz:
-            lz_step(k + 2, lz_of(k)).start()
+    last = nz - 1
+    quarters = (my_y, down_q, up_q, far_q)
+
+    def lz_step(k, j, source):
+        q = quarters[j]
+        piece = xw_ref.at[q // 2, :, rows_of(source), late_of(q)]
+        right = j < 2 if k == last else k % 2 == 1
+        return pass_on(piece, (zb_ss, zb_rs), 4 * k + j, to_z(1 if right else nz - 1))
+
+    def lz_begin(j):
+        lz_step(1, j, my_z).start()
+        lz_step(2, j, my_z).start()
+
+    def lz_arrive(level, j):
+        for k in (2 * level - 1, 2 * level):
+            if k < nz:
+                lz_step(k, j, lz_of(k)).wait_recv()
+                if k + 2 < last:
+                    lz_step(k + 2, j, lz_of(k)).start()
+                elif (k == last - 2 and j < 2) or (k == last - 1 and j >= 2):
+                    lz_step(last, j, lz_of(k)).start()
 
     ly_step(my_y, 1, 0).start()
     ly_step(my_y, ny - 1, 1).start()
     z_arrive(0)
+    lz_begin(0)
     ly_step(down_q, 1, 0).wait_recv()
     ly_step(down_q, 1, 2).start()
+    lz_begin(1)
     ly_step(up_q, ny - 1, 1).wait_recv()
+    lz_begin(2)
     z_arrive(1)
     z_arrive(2)
+    lz_arrive(1, 0)
     y_forward(0)
     ly_step(far_q, 1, 2).wait_recv()
-    lz_step(1, my_z).start()
-    lz_step(2, my_z).start()
+    lz_begin(3)
     z_arrive(3)
     z_arrive(4)
-    y_forward(1)
-    z_arrive(5)
-    z_arrive(6)
-    y_forward(2)
-    z_arrive(7)
-    y_forward(3)
-    lz_arrive(1)
-    lz_arrive(2)
-    y_forward(4)
-    y_forward(5)
-    lz_arrive(3)
-    lz_arrive(4)
-    y_forward(6)
-    lz_arrive(5)
-    lz_arrive(6)
-    y_forward(7)
-    lz_arrive(7)
+    for n in range(1, nz):
+        if n == 2:
+            z_arrive(5)
+            z_arrive(6)
+        if n == 3:
+            z_arrive(7)
+        for j in range(4):
+            if 1 <= n + 1 - j <= nz // 2 and (n + 1 - j, j) != (1, 0):
+                lz_arrive(n + 1 - j, j)
+        y_forward(n)
     for k in range(nz):
         y_step(k, far_q, 1, 2).wait_recv()
 
@@ -276,7 +303,8 @@
     for k in range(nz):
         if k:
             z_step(k, z_of(k)).wait_send()
-            lz_step(k, lz_of(k)).wait_send()
+            for j in range(4):
+                lz_step(k, j, lz_of(k)).wait_send()
         for index in range(3):
             y_step(k, my_y, 1, index).wait_send()
     for index in range(3):
@@ -341,10 +369,13 @@
 
     sq_ref[...] = jnp.zeros_like(sq_ref)
 
+    def group_of(n, way=1):
+        m = lax.rem(n, 4)
+        to = lax.rem(my_y + ny + way * (2 * lax.rem(m, 2) + m // 2), ny)
+        return 2 * to + lax.rem(my_z // 4 + m + 1 + n // 4, 2)
+
     def grad_group(n):
-        m = lax.rem(n, 4)
-        to = lax.rem(my_y + 2 * lax.rem(m, 2) + m // 2, ny)
-        c = 2 * to + lax.rem(my_z // 4 + m + 1 + n // 4, 2)
+        c = group_of(n)
         feats = pl.ds(pl.multiple_of(c * group, group), group)
         total = jnp.zeros(sq_ref.shape, F32)
         first = lax.dot_general(
@@ -361,8 +392,10 @@
                 wide = wide * wide
                 total += jnp.sum(wide.reshape(own // 8, 8, units), axis=0)
         sq_ref[...] += total
+
+    def send_group(n):
         for i in range(4):
-            p = 4 * c + lax.rem(my_z + i, 4)
+            p = 4 * group_of(n) + lax.rem(my_z + i, 4)
 
             @pl.when(p != dp)
             def _():
@@ -370,8 +403,12 @@
 
     def both_kinds(k, _):
         row_pair(k, 0)
-        grad_group(2 * k)
-        grad_group(2 * k + 1)
+        for n in (2 * k, 2 * k + 1):
+            grad_group(n)
+
+            @pl.when(n < EARLY)
+            def _():
+                send_group(n)
         return 0
 
     lax.fori_loop(0, pairs, both_kinds, 0)
@@ -405,15 +442,6 @@
         )
 
     run(1, shards, lambda k: sd_copy(k).start())
-    run(1, shards, lambda k: sd_arrival(k).wait())
-
-    def add_dp(k, total):
-        return total + sq_dp[lax.rem(dp + k, shards)]
-
-    sq_dp[dp] = lax.fori_loop(1, shards, add_dp, sq_ref[...])
-    sq_ex[ex] = sq_dp[dp]
-    run(1, experts, lambda k: se_copy(k).start())
-
     row_recv[ex] = row_send[ex]
 
     def y_copy(k):
@@ -452,6 +480,15 @@
         return 0
 
     lax.fori_loop(1, ny + 1, to_tokens, 0)
+    run(EARLY, EARLY + 1, send_group)
+    run(1, shards, lambda k: sd_arrival(k).wait())
+
+    def add_dp(k, total):
+        return total + sq_dp[lax.rem(dp + k, shards)]
+
+    sq_dp[dp] = lax.fori_loop(1, shards, add_dp, sq_ref[...])
+    sq_ex[ex] = sq_dp[dp]
+    run(1, experts, lambda k: se_copy(k).start())
     y_recv[my_y] = y_send[my_y]
     run(1, ny, lambda k: y_arrival(k).wait())
 
@@ -476,13 +513,8 @@
             total += y_recv[j, rows, :].astype(F32)
         z_send[i] = total.astype(BF16)
     run(1, nz, lambda k: z_copy(k).start())
+    run(EARLY + 1, groups, send_group)
     z_recv[my_z] = z_send[my_z]
-    run(1, nz, lambda k: z_arrival(k).wait())
-    total = z_recv[0].astype(F32)
-    for j in range(1, nz):
-        total += z_recv[j].astype(F32)
-    tok_ref[...] = total.astype(BF16)
-
     run(1, experts, lambda k: se_arrival(k).wait())
     squares = sq_ex[0]
     for j in range(1, experts):
@@ -502,14 +534,23 @@
             grad_send[p, m] = (src[p, m].astype(F32) * scale).astype(BF16)
         out_copy(p).start()
 
+    def finish(n):
+        for i in range(4):
+            p = 4 * group_of(n, -1) + lax.rem(my_z + 4 - i, 4)
+
+            @pl.when(p != dp)
+            def _():
+                grad_arrival(p).wait()
+                clip(grad_recv, p)
+
     clip(grad_send, dp)
-
-    def finish(k):
-        p = lax.rem(dp + shards - k, shards)
-        grad_arrival(p).wait()
-        clip(grad_recv, p)
-
-    run(1, shards, finish)
+    run(0, EARLY, finish)
+    run(1, nz, lambda k: z_arrival(k).wait())
+    total = z_recv[0].astype(F32)
+    for j in range(1, nz):
+        total += z_recv[j].astype(F32)
+    tok_ref[...] = total.astype(BF16)
+    run(EARLY, groups, finish)
     run(0, shards, lambda k: out_copy(k).wait())
 
 
@@ -522,12 +563,6 @@
     slots = experts * CAP
     own = width // shards
 
-    first, second = slot_match(routes, experts)
-    pick = (first | second).astype(BF16)
-    gains = jnp.where(
-        first, gate_values[:, 0][None, :],
-        jnp.where(second, gate_values[:, 1][None, :], jnp.zeros((), BF16)),
-    )
     limit = CLIP_RMS * math.sqrt(3.0 * experts * width * units * shards)
     vmem = pl.BlockSpec(memory_space=pltpu.VMEM)
     dma = pltpu.SemaphoreType.DMA
@@ -540,6 +575,8 @@
         in_specs=[vmem] * 7,
         out_specs=(pl.BlockSpec(memory_space=pl.ANY), vmem),
         scratch_shapes=[
+            pltpu.VMEM((slots, block), BF16),
+            pltpu.VMEM((slots, block), BF16),
             pltpu.VMEM((2, experts, CAP, width), BF16),
             pltpu.VMEM((experts, CAP // nz, (width - DIRECT) // 2), BF16),
             pltpu.VMEM((experts, 2, CAP, DIRECT), BF16),
@@ -558,7 +595,7 @@
             pltpu.VMEM((experts, 8, units), F32),
             dma((2, experts)), dma((2, experts)), dma((experts,)), dma((experts,)),
             dma((nz,)), dma((nz,)), dma((3 * nz,)), dma((3 * nz,)),
-            dma((3,)), dma((3,)), dma((nz,)), dma((nz,)), dma((shards,)),
+            dma((3,)), dma((3,)), dma((4 * nz,)), dma((4 * nz,)), dma((shards,)),
             dma((experts,)), dma((experts,)), dma((shards,)), dma((shards,)),
             dma((ny,)), dma((ny,)), dma((nz,)), dma((nz,)),
             dma((shards,)), dma((shards,)), dma((experts,)), dma((experts,)),
@@ -569,7 +606,7 @@
         cost_estimate=pl.CostEstimate(
             flops=16 * slots * width * units, bytes_accessed=30_000_000, transcendentals=slots * units
         ),
-    )(tokens, cotangent, pick, gains, gate_weight[0], up_weight[0], down_weight[0])
+    )(tokens, cotangent, routes.T, gate_values.T, gate_weight[0], up_weight[0], down_weight[0])
     return clipped[None], d_tokens
 
 

time: 245 us -> 214 us (0.87)
  the two profiles are of different devices: /device:TPU:2 before, /device:TPU:12 now
where the time goes in v4:
time: 214 us; the launch traced here: 211 us
  Pallas kernels  204 us (95%)
  local copies, waits for them, and re-layouts  5.66 us (3%)
    pallas_call x1, Pallas kernels, per_device(): pl.pallas_call(functools.partial(kernel, (ny, nz, experts, limit)), out_s...  204 us
    unnamed x4, local copies, waits for them, and re-layouts  5.66 us

profile of v4, /device:TPU:12, one launch (start us, length us, event | category | flops | bytes accessed | tf_op | source)
XLA Modules:
  0.0 210.5 jit_solution(588899208783521764)
XLA Ops:
  0.6 204.2 %shard_map.86 = (bf16[3,96,8192]{2,1,0:T(8,128)(2,1)}, bf16[96,256]{1,0:T(8,128)(2,1)}) custom-call(bf16[256,3072]{1,0:T(8,128)(2,1)} %tok_in.1, bf16[256,3072]{1,0:T(8,128)(2,1)} %cot_in.1, s32[2,256]{1,0:T(2,128)} %bitcast.10, bf16[2,256]{1,0:T(2,128)(2,1)} %bitcast.11, bf16[3072,256]{1,0:T(8,128)(2,1)} %bitcast.7, bf16[3072,256]{1,0:T(8,128)(2,1)} %bitcast.8, ...), custom_call_target="tpu_custom_call" | custom-call | flops 12884901888 | bytes 30000000 | tf_op jit(solution)/shard_map/pallas_call | solution.py:569
  204.8 0.0 copy-start
  204.9 5.0 %copy.11 = bf16[1,3,96,8192]{3,2,1,0:T(8,128)(2,1)} copy(bf16[1,3,96,8192]{3,2,1,0:T(8,128)(2,1)} %bitcast.6) | data formatting | bytes 9437184
  209.9 0.0 copy-done
  209.9 0.6 copy.12
Async XLA Ops:
  204.8 5.1 %copy-start = (bf16[96,256]{1,0:T(8,128)(2,1)S(1)}, bf16[96,256]{1,0:T(8,128)(2,1)}, u32[]{:S(2)}) copy-start(bf16[96,256]{1,0:T(8,128)(2,1)} %get-tuple-element.9) | copy-start | bytes 147460

commit v5 on v4

--- a/solution.py
+++ b/solution.py
@@ -11,7 +11,7 @@
 CAP = 128
 CLIP_RMS = 0.2
 DIRECT = 1024
-BAND = 640
+BAND = 768
 EARLY = 7
 MESH = pl.DeviceIdType.MESH
 F32 = jnp.float32
@@ -47,11 +47,11 @@
 
 def kernel(
     shape,
-    tok_in, cot_in, routes_ref, gates_ref, gate_ref, up_ref, down_ref,
+    tok_in, cot_in, routes_ref, gates_ref, gate_in, up_in, down_in,
     clip_ref, tok_ref,
-    pick_ref, gain_ref, xw_ref, piece_send, direct_send, h_ref, g_ref, row_send, row_recv, grad_send, grad_recv,
+    gate_ref, up_ref, down_ref, pick_ref, gain_ref, xw_ref, piece_send, direct_send, h_ref, g_ref, row_send, row_recv, grad_send, grad_recv,
     y_send, y_recv, z_send, z_recv, sq_ref, sq_dp, sq_ex,
-    piece_ss, piece_rs, direct_ss, direct_rs, za_ss, za_rs, ya_ss, ya_rs, yb_ss, yb_rs, zb_ss, zb_rs, out_sem,
+    weight_sem, piece_ss, piece_rs, direct_ss, direct_rs, za_ss, za_rs, ya_ss, ya_rs, yb_ss, yb_rs, zb_ss, zb_rs, out_sem,
     row_ss, row_rs, grad_ss, grad_rs, y_ss, y_rs, z_ss, z_rs, sd_ss, sd_rs, se_ss, se_rs,
 ):
     ny, nz, experts, limit = shape
@@ -62,34 +62,49 @@
     slots = pick_ref.shape[0]
     width = tok_in.shape[1]
     units = gate_ref.shape[1]
-    own = width // shards
-    group = own * 4
-    groups = shards // 4
-    tile = slots // experts
-
-    barrier = pltpu.get_barrier_semaphore()
-
-    def greet_dp(k, _):
-        pl.semaphore_signal(
-            barrier, inc=1, device_id=(lax.rem(dp + k, shards), ex), device_id_type=MESH
-        )
-        return 0
-
-    def greet_ex(k, _):
-        pl.semaphore_signal(
-            barrier, inc=1, device_id=(dp, lax.rem(ex + k, experts)), device_id_type=MESH
-        )
-        return 0
-
-    lax.fori_loop(1, shards, greet_dp, 0)
-    lax.fori_loop(1, experts, greet_ex, 0)
-    fill_slots(routes_ref, gates_ref, pick_ref, gain_ref, experts)
 
     def run(first, count, do):
         def body(k, _):
             do(k)
             return 0
         lax.fori_loop(first, count, body, 0)
+
+    weights = (
+        pltpu.make_async_copy(gate_in, gate_ref, weight_sem.at[0]),
+        pltpu.make_async_copy(up_in, up_ref, weight_sem.at[1]),
+        pltpu.make_async_copy(down_in, down_ref, weight_sem.at[2]),
+    )
+    for copy in weights:
+        copy.start()
+    own = width // shards
+    group = own * 4
+    groups = shards // 4
+    tile = slots // experts
+
+    barrier = pltpu.get_barrier_semaphore()
+
+    def greet_dp(k, _):
+        pl.semaphore_signal(
+            barrier, inc=1, device_id=(lax.rem(dp + k, shards), ex), device_id_type=MESH
+        )
+        return 0
+
+    def greet_ex(k, _):
+        pl.semaphore_signal(
+            barrier, inc=1, device_id=(dp, lax.rem(ex + k, experts)), device_id_type=MESH
+        )
+        return 0
+
+    for way in (1, ny - 1):
+        pl.semaphore_signal(
+            barrier, inc=1, device_id=(lax.rem(my_y + way, ny) * nz + my_z, ex), device_id_type=MESH
+        )
+    for way in (1, nz - 1):
+        pl.semaphore_signal(
+            barrier, inc=1, device_id=(my_y * nz + lax.rem(my_z + way, nz), ex), device_id_type=MESH
+        )
+    lax.fori_loop(1, experts, greet_ex, 0)
+    fill_slots(routes_ref, gates_ref, pick_ref, gain_ref, experts)
 
     direct = direct_send.shape[-1]
     half, late = BAND, (width - direct) // 2 - BAND
@@ -127,46 +142,39 @@
     def _():
         make_piece(gain_ref, cot_in)
 
-    pl.semaphore_wait(barrier, shards + experts - 2)
-
-    def piece_copy(e, b, m):
-        cols = cols_of(my_y) if m == 0 else late_of(my_y)
-        return pltpu.make_async_remote_copy(
-            src_ref=piece_send.at[e, :, pl.ds(0, half) if m == 0 else pl.ds(half, late)],
-            dst_ref=xw_ref.at[my_array, b, rows_of(my_z), cols],
-            send_sem=piece_ss.at[m, e], recv_sem=piece_rs.at[m, b],
-            device_id=(dp, e), device_id_type=MESH,
-        )
-
-    def send_piece(k):
-        for m in (1, 0):
-            piece_copy(lax.rem(ex + k, experts), ex, m).start()
-
-    run(1, experts, send_piece)
-    xw_ref[my_array, ex, rows_of(my_z), cols_of(my_y)] = piece_send[ex, :, :half]
-    xw_ref[my_array, ex, rows_of(my_z), late_of(my_y)] = piece_send[ex, :, half:]
-
-    def direct_copy(e, b):
-        return pltpu.make_async_remote_copy(
-            src_ref=direct_send.at[e], dst_ref=xw_ref.at[:, b, :, pl.ds(0, direct)],
-            send_sem=direct_ss.at[e], recv_sem=direct_rs.at[b], device_id=(dp, e), device_id_type=MESH,
-        )
-
-    def make_direct(k, _):
-        e = lax.rem(ex + k, experts)
+    def make_direct(e):
         rows = pl.ds(pl.multiple_of(e * tile, tile), tile)
         for m, (select_ref, values_ref) in enumerate(((pick_ref, tok_in), (gain_ref, cot_in))):
             direct_send[e, m] = jnp.dot(
                 select_ref[rows, :], values_ref[:, :direct], preferred_element_type=F32
             ).astype(BF16)
 
-        @pl.when(e != ex)
-        def _():
-            direct_copy(e, ex).start()
-        return 0
-
-    lax.fori_loop(1, experts + 1, make_direct, 0)
-    xw_ref[:, ex, :, :direct] = direct_send[ex]
+    run(0, experts, make_direct)
+    pl.semaphore_wait(barrier, experts + 3)
+
+    def piece_copy(e, b, m):
+        cols = cols_of(my_y) if m == 0 else late_of(my_y)
+        return pltpu.make_async_remote_copy(
+            src_ref=piece_send.at[e, :, pl.ds(0, half) if m == 0 else pl.ds(half, late)],
+            dst_ref=xw_ref.at[my_array, b, rows_of(my_z), cols],
+            send_sem=piece_ss.at[m, e], recv_sem=piece_rs.at[m, b],
+            device_id=(dp, e), device_id_type=MESH,
+        )
+
+    def send_piece(k):
+        for m in (1, 0):
+            piece_copy(lax.rem(ex + k, experts), ex, m).start()
+
+    run(1, experts, send_piece)
+    xw_ref[my_array, ex, rows_of(my_z), cols_of(my_y)] = piece_send[ex, :, :half]
+    xw_ref[my_array, ex, rows_of(my_z), late_of(my_y)] = piece_send[ex, :, half:]
+
+    def direct_copy(e, b):
+        return pltpu.make_async_remote_copy(
+            src_ref=direct_send.at[e], dst_ref=xw_ref.at[:, b, :, pl.ds(0, direct)],
+            send_sem=direct_ss.at[e], recv_sem=direct_rs.at[b], device_id=(dp, e), device_id_type=MESH,
+        )
+
 
     def wait_piece(k):
         e = lax.rem(ex + k, experts)
@@ -250,6 +258,8 @@
     ly_step(my_y, ny - 1, 1).start()
     z_arrive(0)
     lz_begin(0)
+    run(1, experts, lambda k: direct_copy(lax.rem(ex + k, experts), ex).start())
+    xw_ref[:, ex, :, :direct] = direct_send[ex]
     ly_step(down_q, 1, 0).wait_recv()
     ly_step(down_q, 1, 2).start()
     lz_begin(1)
@@ -282,6 +292,10 @@
 
     run(1, experts, wait_direct)
 
+    lax.fori_loop(1, shards, greet_dp, 0)
+    for copy in weights:
+        copy.wait()
+
     def hidden(i, _):
         rows = pl.ds(pl.multiple_of(i * 2 * tile, 2 * tile), 2 * tile)
         x = xw_ref[0, pl.ds(2 * i, 2)].reshape(2 * tile, width)
@@ -403,8 +417,14 @@
 
     def both_kinds(k, _):
         row_pair(k, 0)
-        for n in (2 * k, 2 * k + 1):
+        for i in range(2):
+            n = 2 * k + i
             grad_group(n)
+            if i == 0:
+
+                @pl.when(k == 0)
+                def _():
+                    pl.semaphore_wait(barrier, shards - 1)
 
             @pl.when(n < EARLY)
             def _():
@@ -572,9 +592,12 @@
             jax.ShapeDtypeStruct((3, own, units * shards), BF16),
             jax.ShapeDtypeStruct((own, block), BF16),
         ),
-        in_specs=[vmem] * 7,
+        in_specs=[vmem] * 4 + [pl.BlockSpec(memory_space=pl.ANY)] * 3,
         out_specs=(pl.BlockSpec(memory_space=pl.ANY), vmem),
         scratch_shapes=[
+            pltpu.VMEM((width, units), BF16),
+            pltpu.VMEM((width, units), BF16),
+            pltpu.VMEM((width, units), BF16),
             pltpu.VMEM((slots, block), BF16),
             pltpu.VMEM((slots, block), BF16),
             pltpu.VMEM((2, experts, CAP, width), BF16),
@@ -593,7 +616,7 @@
             pltpu.VMEM((8, units), F32),
             pltpu.VMEM((shards, 8, units), F32),
             pltpu.VMEM((experts, 8, units), F32),
-            dma((2, experts)), dma((2, experts)), dma((experts,)), dma((experts,)),
+            dma((3,)), dma((2, experts)), dma((2, experts)), dma((experts,)), dma((experts,)),
             dma((nz,)), dma((nz,)), dma((3 * nz,)), dma((3 * nz,)),
             dma((3,)), dma((3,)), dma((4 * nz,)), dma((4 * nz,)), dma((shards,)),
             dma((experts,)), dma((experts,)), dma((shards,)), dma((shards,)),

time: 214 us -> 212 us (level)
  no operation moved by 1% of the time
where the time goes in v5:
time: 212 us; the launch traced here: 210 us
  Pallas kernels  204 us (96%)
  local copies, waits for them, and re-layouts  5.66 us (3%)
    pallas_call x1, Pallas kernels, per_device(): pl.pallas_call(functools.partial(kernel, (ny, nz, experts, limit)), out_s...  204 us
    unnamed x4, local copies, waits for them, and re-layouts  5.66 us

profile of v5, /device:TPU:12, one launch (start us, length us, event | category | flops | bytes accessed | tf_op | source)
XLA Modules:
  0.0 209.9 jit_solution(2440262026481086772)
XLA Ops:
  0.6 203.6 %shard_map.86 = (bf16[3,96,8192]{2,1,0:T(8,128)(2,1)}, bf16[96,256]{1,0:T(8,128)(2,1)}) custom-call(bf16[256,3072]{1,0:T(8,128)(2,1)} %tok_in.1, bf16[256,3072]{1,0:T(8,128)(2,1)} %cot_in.1, s32[2,256]{1,0:T(2,128)} %bitcast.10, bf16[2,256]{1,0:T(2,128)(2,1)} %bitcast.11, bf16[3072,256]{1,0:T(8,128)(2,1)} %bitcast.7, bf16[3072,256]{1,0:T(8,128)(2,1)} %bitcast.8, ...), custom_call_target="tpu_custom_call" | custom-call | flops 12884901888 | bytes 30000000 | tf_op jit(solution)/shard_map/pallas_call | solution.py:589
  204.2 0.0 copy-start
  204.2 5.0 %copy.11 = bf16[1,3,96,8192]{3,2,1,0:T(8,128)(2,1)} copy(bf16[1,3,96,8192]{3,2,1,0:T(8,128)(2,1)} %bitcast.6) | data formatting | bytes 9437184
  209.2 0.0 copy-done
  209.3 0.6 copy.12
Async XLA Ops:
  204.2 5.1 %copy-start = (bf16[96,256]{1,0:T(8,128)(2,1)S(1)}, bf16[96,256]{1,0:T(8,128)(2,1)}, u32[]{:S(2)}) copy-start(bf16[96,256]{1,0:T(8,128)(2,1)} %get-tuple-element.9) | copy-start | bytes 147460

commit v6 on v5

--- a/solution.py
+++ b/solution.py
@@ -415,23 +415,23 @@
             def _():
                 grad_copy(p).start()
 
-    def both_kinds(k, _):
-        row_pair(k, 0)
-        for i in range(2):
-            n = 2 * k + i
-            grad_group(n)
-            if i == 0:
-
-                @pl.when(k == 0)
-                def _():
-                    pl.semaphore_wait(barrier, shards - 1)
-
-            @pl.when(n < EARLY)
-            def _():
-                send_group(n)
+    def both_kinds(n, _):
+        @pl.when(n < pairs)
+        def _():
+            row_pair(n, 0)
+
+        grad_group(n)
+
+        @pl.when(n == 0)
+        def _():
+            pl.semaphore_wait(barrier, shards - 1)
+
+        @pl.when(n < EARLY)
+        def _():
+            send_group(n)
         return 0
 
-    lax.fori_loop(0, pairs, both_kinds, 0)
+    lax.fori_loop(0, groups, both_kinds, 0)
 
     def sd_copy(k):
         p = lax.rem(dp + k, shards)

time: 212 us -> 211 us (level)
  no operation moved by 1% of the time
where the time goes in v6:
time: 211 us; the launch traced here: 209 us
  Pallas kernels  203 us (96%)
  local copies, waits for them, and re-layouts  5.66 us (3%)
    pallas_call x1, Pallas kernels, per_device(): pl.pallas_call(functools.partial(kernel, (ny, nz, experts, limit)), out_s...  203 us
    unnamed x4, local copies, waits for them, and re-layouts  5.66 us

profile of v6, /device:TPU:12, one launch (start us, length us, event | category | flops | bytes accessed | tf_op | source)
XLA Modules:
  0.0 209.1 jit_solution(13890908525295719616)
XLA Ops:
  0.6 202.7 %shard_map.86 = (bf16[3,96,8192]{2,1,0:T(8,128)(2,1)}, bf16[96,256]{1,0:T(8,128)(2,1)}) custom-call(bf16[256,3072]{1,0:T(8,128)(2,1)} %tok_in.1, bf16[256,3072]{1,0:T(8,128)(2,1)} %cot_in.1, s32[2,256]{1,0:T(2,128)} %bitcast.10, bf16[2,256]{1,0:T(2,128)(2,1)} %bitcast.11, bf16[3072,256]{1,0:T(8,128)(2,1)} %bitcast.7, bf16[3072,256]{1,0:T(8,128)(2,1)} %bitcast.8, ...), custom_call_target="tpu_custom_call" | custom-call | flops 12884901888 | bytes 30000000 | tf_op jit(solution)/shard_map/pallas_call | solution.py:589
  203.4 0.0 copy-start
  203.4 5.0 %copy.11 = bf16[1,3,96,8192]{3,2,1,0:T(8,128)(2,1)} copy(bf16[1,3,96,8192]{3,2,1,0:T(8,128)(2,1)} %bitcast.6) | data formatting | bytes 9437184
  208.4 0.0 copy-done
  208.4 0.6 copy.12
Async XLA Ops:
  203.4 5.1 %copy-start = (bf16[96,256]{1,0:T(8,128)(2,1)S(1)}, bf16[96,256]{1,0:T(8,128)(2,1)}, u32[]{:S(2)}) copy-start(bf16[96,256]{1,0:T(8,128)(2,1)} %get-tuple-element.9) | copy-start | bytes 147460
